TPU v7x, 32 devices: a whole 2x2x4 slice. The times are simulated.
32 devices in a mesh: section: 2 (over core), dp: 16 (over z, y, x).
Axes of the slice: x: 2, y: 2, z: 4, core: 2. Of those that a mesh axis runs over, the one named last changes fastest.
Arguments:
- clips: bfloat16 [8, 16, 4, 8, 8, 128], P(None, 'dp'), may hold values from -6 to 6
- cotangent: bfloat16 [8, 16, 4, 8, 8, 128], P(None, 'dp'), may hold values from -6 to 6
- weights: bfloat16 [2, 3456, 128], P('section', 'dp'), may hold values from -0.078125 to 0.078125
Outputs:
- section_outs: bfloat16 [2, 8, 16, 4, 8, 8, 128], P('section', None, 'dp')
- weight_grads: float32 [2, 3456, 128], P('section', 'dp')
All inputs are finite; a program needn't handle non-finite values.
Results may differ from a plain program's by a relative error of at most 0.027.
Values may be sent and summed in bfloat16 or wider, within the bound.
No kernel may reach another device: no remote copies, remote signals or barrier semaphores. Data moves between devices by JAX's collectives and lax.ppermute only.
A program may use at most 64 MiB of HBM per device.

v0:
```python
import functools

import jax
import jax.numpy as jnp
from jax import lax
from jax.experimental import pallas as pl
from jax.experimental.pallas import tpu as pltpu
from jax.sharding import PartitionSpec as P


def passed_along(block, axis, distance):
    devices = range(lax.axis_size(axis))
    route = [(i - distance, i) for i in devices if i - distance in devices]
    return lax.ppermute(block, axis, route)


def gather_patches(field):
    frames, height, width, channels = field.shape
    first_frame = field[:1]
    padded = jnp.concatenate([first_frame, first_frame, field], axis=0)
    padded = jnp.pad(padded, ((0, 0), (1, 1), (1, 1), (0, 0)))
    pieces = [
        padded[
            offset_time : offset_time + frames,
            offset_row : offset_row + height,
            offset_col : offset_col + width,
        ]
        for offset_time in range(3)
        for offset_row in range(3)
        for offset_col in range(3)
    ]
    return jnp.stack(pieces, axis=3).reshape(frames * height * width, 27 * channels)


def squash_field(activation):
    return jax.nn.silu(activation.astype(jnp.float32)).astype(jnp.bfloat16)


def squash_columns(activation):
    return gather_patches(squash_field(activation))


def layer_forward(activation, weight):
    branch = jnp.dot(squash_columns(activation), weight, preferred_element_type=jnp.float32)
    return (activation.astype(jnp.float32) + branch.reshape(activation.shape)).astype(jnp.bfloat16)


def input_gradient(activation, upstream, weight):
    flat_grad = upstream.reshape(-1, weight.shape[1])
    column_grad = lax.dot_general(
        flat_grad, weight, (((1,), (1,)), ((), ())), preferred_element_type=jnp.float32
    )
    base = activation.astype(jnp.float32)
    _, unfold = jax.vjp(gather_patches, base)
    field_grad = unfold(column_grad)[0]
    sigmoid_value = jax.nn.sigmoid(base)
    slope = sigmoid_value * (1.0 + base * (1.0 - sigmoid_value))
    return (upstream.astype(jnp.float32) + field_grad * slope).astype(jnp.bfloat16)


def weight_term(activation, upstream):
    flat_grad = upstream.reshape(-1, upstream.shape[-1])
    return lax.dot_general(
        squash_columns(activation),
        flat_grad,
        (((0,), (0,)), ((), ())),
        preferred_element_type=jnp.float32,
    )


def many_sections(clips, cotangent, weights):
    section_total = lax.axis_size("section")
    section_index = lax.axis_index("section")
    weight = lax.all_gather(weights, "dp", axis=1, tiled=True)[0]
    local_clips = clips[:, 0]
    local_grads = cotangent[:, 0]
    micro_count = local_clips.shape[0]
    step_count = micro_count + section_total - 1
    empty_field = jnp.zeros(local_clips.shape[1:], jnp.bfloat16)

    def forward_step(step_index, carry):
        received, saved_inputs, produced = carry
        micro_index = step_index - section_index
        active = (micro_index >= 0) & (micro_index < micro_count)
        slot_index = jnp.clip(micro_index, 0, micro_count - 1)
        fresh = lax.dynamic_index_in_dim(local_clips, slot_index, 0, keepdims=False)
        layer_input = jnp.where(section_index == 0, fresh, received)
        layer_output = layer_forward(layer_input, weight)
        kept_input = jnp.where(
            active,
            layer_input,
            lax.dynamic_index_in_dim(saved_inputs, slot_index, 0, keepdims=False),
        )
        kept_output = jnp.where(
            active, layer_output, lax.dynamic_index_in_dim(produced, slot_index, 0, keepdims=False)
        )
        saved_inputs = lax.dynamic_update_index_in_dim(saved_inputs, kept_input, slot_index, 0)
        produced = lax.dynamic_update_index_in_dim(produced, kept_output, slot_index, 0)
        received = passed_along(layer_output, "section", 1)
        return (received, saved_inputs, produced)

    start_forward = (empty_field, jnp.zeros_like(local_clips), jnp.zeros_like(local_clips))
    _, saved_inputs, produced = lax.fori_loop(0, step_count, forward_step, start_forward)

    def backward_step(step_index, carry):
        received, grad_total, kept_grads = carry
        micro_index = step_index - (section_total - 1 - section_index)
        active = (micro_index >= 0) & (micro_index < micro_count)
        slot_index = jnp.clip(micro_index, 0, micro_count - 1)
        fresh = lax.dynamic_index_in_dim(local_grads, slot_index, 0, keepdims=False)
        upstream = jnp.where(section_index == section_total - 1, fresh, received)
        activation = lax.dynamic_index_in_dim(saved_inputs, slot_index, 0, keepdims=False)
        grad_total = grad_total + jnp.where(active, weight_term(activation, upstream), 0.0)
        layer_grad = input_gradient(activation, upstream, weight)
        received = passed_along(layer_grad, "section", -1)
        return (received, grad_total, kept_grads)

    start_backward = (
        empty_field,
        jnp.zeros(weight.shape, jnp.float32),
        jnp.zeros_like(local_grads),
    )
    _, grad_total, kept_grads = lax.fori_loop(0, step_count, backward_step, start_backward)
    grad_share = lax.psum_scatter(
        grad_total.astype(jnp.bfloat16), "dp", scatter_dimension=0, tiled=True
    ).astype(jnp.float32)
    return (produced[None, :, None], grad_share[None])


def summed(terms):
    return functools.reduce(lambda p, q: p + q, terms)


def frame_of(halves, t):
    return halves[t // halves[0].shape[0]].at[t % halves[0].shape[0]]


def silu_of(value):
    return value * jax.nn.sigmoid(value)


def slope_of(value):
    sigmoid_value = jax.nn.sigmoid(value)
    return sigmoid_value * (1.0 + value * (1.0 - sigmoid_value))


def column_shifts(rows, width):
    height, flat, channels = rows.shape
    cells = rows.reshape(height * flat // width, width, channels)
    column = lax.broadcasted_iota(jnp.int32, cells.shape, 1)
    before = jnp.where(column == 0, 0.0, pltpu.roll(cells, 1, 1))
    after = jnp.where(column == width - 1, 0.0, pltpu.roll(cells, width - 1, 1))
    return [piece.reshape(rows.shape).astype(jnp.bfloat16) for piece in (before, cells, after)]


def whole(count):
    return [pl.BlockSpec(memory_space=pltpu.VMEM)] * count


def call(body, inputs, outputs, scratch, flops, far=False):
    return pl.pallas_call(
        body,
        out_shape=[jax.ShapeDtypeStruct(shape, dtype) for shape, dtype in outputs],
        in_specs=[pl.BlockSpec(memory_space=pl.ANY)] * len(inputs) if far else whole(len(inputs)),
        out_specs=whole(len(outputs)),
        scratch_shapes=scratch,
        compiler_params=pltpu.CompilerParams(vmem_limit_bytes=32 * 1024 * 1024),
        cost_estimate=pl.CostEstimate(flops=flops, bytes_accessed=4_000_000, transcendentals=0),
    )(*inputs)


def turn_into(turned, k, t, piece):
    channels = piece.shape[-1]
    flat = piece.reshape(-1, channels)
    cells = flat.shape[0]
    turned[k * channels : (k + 1) * channels, t * cells : (t + 1) * cells] = flat.T


def pad_rows(grads):
    count, padded_height, flat, channels = grads.shape
    zero_row = jnp.zeros((count, 1, flat, channels), jnp.bfloat16)
    grads[:, :1] = zero_row
    grads[:, padded_height - 1 :] = zero_row


def place_grads(grads, fields):
    height = fields[0].shape[0]
    first_two = fields[0] + fields[1]
    for t, field in enumerate((*fields, first_two, first_two + fields[2])):
        grads[t, 1 : height + 1] = field.astype(jnp.bfloat16)


def copy_body(source, target):
    target[...] = source[...]


def prepare_body(clips_far, cotangent_far, *refs):
    shifted, base, upstream, ready, held, clips, cotangent, sems = refs
    micro, frames, height, width, channels = clips.shape
    section = lax.axis_index("section")
    copies = [
        pltpu.make_async_copy(source, target, sems.at[k])
        for k, (source, target) in enumerate(
            ((clips_far, clips), (cotangent_far, cotangent))
        )
    ]
    for copy in copies:
        copy.start()

    def reorder(source, target):
        for m in range(micro):
            held[:, :, m * width : (m + 1) * width, :] = source[m].astype(jnp.float32)
        for t in range(frames):
            target[t] = held[t].astype(jnp.bfloat16)

    zero_row = jnp.zeros((3, frames, 1) + shifted.shape[3:], jnp.bfloat16)
    shifted[:, :, :1] = zero_row
    shifted[:, :, height + 1 :] = zero_row
    copies[0].wait()
    reorder(clips, base)
    copies[1].wait()
    reorder(cotangent, upstream)

    @pl.when(section == 0)
    def _():
        for t in range(frames):
            squashed = silu_of(base[t].astype(jnp.float32)).astype(jnp.bfloat16)
            for k, piece in enumerate(column_shifts(squashed.astype(jnp.float32), width)):
                shifted[k, t, 1 : height + 1] = piece
                turn_into(ready, k, t, piece)

    @pl.when(section != 0)
    def _():
        for t in range(frames):
            for k, piece in enumerate(column_shifts(upstream[t].astype(jnp.float32), width)):
                shifted[k, t, 1 : height + 1] = piece


def shard_rows(rows, first, second):
    section, index = lax.axis_index("section"), lax.axis_index("dp")
    far, near = jnp.where(section == 0, first, second), jnp.where(section == 0, second, first)
    return pl.ds(pl.multiple_of((index ^ (4 * far + near)) * rows, 8), rows)


def unpack_weights(blocks, table):
    rows = blocks[0].shape[1]
    for second in range(4):
        for first in range(4):
            shard = blocks[second][first]
            table[shard_rows(rows, first, second), :] = shard.astype(jnp.float32)


def forward_weights(table, channels):
    rows = 9 * channels
    return jnp.concatenate(
        [table[t * rows : (t + 1) * rows, :].astype(jnp.bfloat16) for t in range(3)], axis=1
    )


def backward_weights(table, channels):
    def turned_taps(times):
        blocks = []
        for k in reversed(range(9)):
            rows = [table[(t * 9 + k) * channels : (t * 9 + k + 1) * channels, :] for t in times]
            blocks.append(summed(rows).astype(jnp.bfloat16))
        return jnp.concatenate(blocks, axis=1)

    return [turned_taps(times) for times in ((0,), (1,), (2,), (0, 1), (0, 1, 2))]


def row_patches(shifted, start, count, height):
    flat, channels = shifted.shape[3:]
    return jnp.concatenate(
        [
            shifted[k, start : start + count, e : e + height].reshape(count * height * flat, channels)
            for e in range(3)
            for k in range(3)
        ],
        axis=1,
    )


def forward_product(shifted, weights, frames, height):
    channels = shifted.shape[-1]
    cells = height * shifted.shape[-2]
    pieces = {}
    for start, count, first_tap in ((0, frames - 2, 0), (frames - 2, 1, 1), (frames - 1, 1, 2)):
        part = jnp.dot(
            row_patches(shifted, start, count, height),
            weights[:, first_tap * channels :],
            preferred_element_type=jnp.float32,
        )
        for t in range(start, start + count):
            rows = slice((t - start) * cells, (t - start + 1) * cells)
            for tap in range(first_tap, 3):
                columns = slice((tap - first_tap) * channels, (tap - first_tap + 1) * channels)
                pieces[t, tap] = part[rows, columns]
    return [
        summed([pieces[max(t + tap - 2, 0), tap] for tap in range(3)]) for t in range(frames)
    ]


def backward_product(shifted, weights, frames, height):
    channels = shifted.shape[-1]
    cells = height * shifted.shape[-2]
    first, second, third, first_two, all_three = weights
    plan = (
        (2, frames - 2, ((first, -2), (second, -1), (third, 0))),
        (1, 1, ((third, 0), (first_two, -1))),
        (0, 1, ((all_three, 0),)),
    )
    reaching = [[] for _ in range(frames)]
    for start, count, terms in plan:
        part = lax.dot_general(
            row_patches(shifted, start, count, height),
            jnp.concatenate([weight for weight, _ in terms], axis=0),
            (((1,), (1,)), ((), ())),
            preferred_element_type=jnp.float32,
        )
        for t in range(start, start + count):
            rows = slice((t - start) * cells, (t - start + 1) * cells)
            for column, (_, step) in enumerate(terms):
                reaching[t + step].append(part[rows, column * channels : (column + 1) * channels])
    return [summed(terms) for terms in reaching]


def first_body(*refs):
    blocks = refs[:4]
    shifted, base, *results, table = refs[4:]
    frames, height, flat, channels = base.shape
    section = lax.axis_index("section")
    unpack_weights(blocks, table)

    @pl.when(section == 0)
    def _():
        branch = forward_product(shifted, forward_weights(table, channels), frames, height)
        for t in range(frames):
            total = base[t].astype(jnp.float32) + branch[t].reshape(height, flat, channels)
            frame_of(results, t)[...] = total.astype(jnp.bfloat16)

    @pl.when(section != 0)
    def _():
        branch = backward_product(shifted, backward_weights(table, channels), frames, height)
        for t in range(frames):
            frame_of(results, t)[...] = branch[t].reshape(height, flat, channels).astype(jnp.bfloat16)


def between_body(mine_low, mine_high, upstream, slope, grads):
    frames = upstream.shape[0]

    @pl.when(lax.axis_index("section") == 0)
    def _():
        for t in range(frames):
            slope[t] = slope_of(frame_of((mine_low, mine_high), t)[...].astype(jnp.float32))

    @pl.when(lax.axis_index("section") != 0)
    def _():
        pad_rows(grads)
        place_grads(grads, [upstream[t].astype(jnp.float32) for t in range(frames)])


def second_body(width, ready, slope, moved, other_low, other_high, upstream, *refs):
    shares, turned, grads = refs
    frames, height, flat, channels = upstream.shape
    rows = shares.shape[2]
    section = lax.axis_index("section")
    cells = height * flat

    def product(left, right):
        taps, done = [], 0
        for met in ((frames + 1, 3), (frames, 2, 3), (0, 1, 2, 3)):
            columns = jnp.concatenate(
                [
                    jnp.concatenate(
                        [
                            right[f, 2 - e : 2 - e + height].reshape(cells, channels)
                            for e in range(3)
                        ],
                        axis=1,
                    )
                    for f in met
                ],
                axis=0,
            )
            part = jnp.dot(
                left[:, : len(met) * cells], columns, preferred_element_type=jnp.float32
            )
            for e in range(3):
                for k in range(3):
                    taps.append(
                        part[k * channels : (k + 1) * channels, e * channels : (e + 1) * channels]
                    )
            while (done + 1) * rows <= len(taps) * channels:
                pieces, row = [], done * rows
                while row < (done + 1) * rows:
                    tap_of, low = divmod(row, channels)
                    high = min(channels, low + (done + 1) * rows - row)
                    pieces.append(taps[tap_of][low:high])
                    row += high - low
                bits = lax.axis_index("dp") ^ done
                far, near = bits // 4, bits % 4
                first = jnp.where(section == 0, far, near)
                second = jnp.where(section == 0, near, far)
                shares[second, first] = jnp.concatenate(pieces, axis=0).astype(jnp.bfloat16)
                done += 1

    @pl.when(section == 0)
    def _():
        pad_rows(grads)
        values = [
            upstream[t].astype(jnp.float32) + slope[t] * frame_of((other_low, other_high), t)[...].astype(jnp.float32)
            for t in range(frames)
        ]
        place_grads(grads, [value.astype(jnp.bfloat16).astype(jnp.float32) for value in values])
        product(ready, grads)

    @pl.when(section != 0)
    def _():
        for t in range(frames):
            squashed = silu_of(frame_of((other_low, other_high), t)[...].astype(jnp.float32)).astype(jnp.bfloat16)
            for k, piece in enumerate(column_shifts(squashed.astype(jnp.float32), width)):
                turn_into(turned, k, t, piece)
        product(turned, moved)


def third_body(*refs):
    blocks = refs[:4]
    mine, other, (produced, table, shifted) = refs[4:6], refs[6:8], refs[8:]
    micro, frames, height, width, channels = produced.shape
    flat = micro * width
    section = lax.axis_index("section")

    def hand_out(t, cells):
        for m in range(micro):
            produced[m, t] = cells[:, m * width : (m + 1) * width, :].astype(jnp.bfloat16)

    @pl.when(section == 0)
    def _():
        for t in range(frames):
            hand_out(t, frame_of(mine, t)[...].astype(jnp.float32))

    @pl.when(section != 0)
    def _():
        unpack_weights(blocks, table)
        zero_row = jnp.zeros((3, frames, 1, flat, channels), jnp.bfloat16)
        shifted[:, :, :1] = zero_row
        shifted[:, :, height + 1 :] = zero_row
        for t in range(frames):
            squashed = silu_of(frame_of(other, t)[...].astype(jnp.float32)).astype(jnp.bfloat16)
            for k, piece in enumerate(column_shifts(squashed.astype(jnp.float32), width)):
                shifted[k, t, 1 : height + 1] = piece
        branch = forward_product(shifted, forward_weights(table, channels), frames, height)
        for t in range(frames):
            hand_out(t, frame_of(other, t)[...].astype(jnp.float32) + branch[t].reshape(height, flat, channels))


def paired_sections(clips, cotangent, weights):
    dp_total = lax.axis_size("dp")
    local_clips, local_grads, shard = clips[:, 0], cotangent[:, 0], weights[0]
    micro, frames, height, width, channels = local_clips.shape
    rows = shard.shape[0]
    flat = micro * width
    cells = height * flat

    def traded(block, along_z, step):
        bits = (4 * step, step) if along_z else (step, 4 * step)
        route = [
            (s * dp_total + i, s * dp_total + (i ^ bits[s])) for s in range(2) for i in range(dp_total)
        ]
        return lax.ppermute(block, ("section", "dp"), route)

    field = (frames, height, flat, channels)
    padded = (3, frames, height + 2, flat, channels)
    met = (frames + 2, height + 2, flat, channels)
    bf16, f32 = jnp.bfloat16, jnp.float32
    unit = 2 * micro * frames * height * width * channels * channels * 27

    first = [traded(shard, True, step) for step in range(1, 4)]
    (shard_copy,) = call(copy_body, (shard,), [(shard.shape, bf16)], [], unit // 16)
    shard_copy, first = lax.optimization_barrier((shard_copy, first))
    line = jnp.stack([shard_copy] + first)
    blocks = (line, *[traded(line, False, step) for step in range(1, 4)])

    turned = (3 * channels, frames * cells)
    shifted, base, upstream, ready = call(
        prepare_body,
        (local_clips, local_grads),
        [(padded, bf16), (field, bf16), (field, bf16), (turned, bf16)],
        [
            pltpu.VMEM(field, f32),
            pltpu.VMEM(local_clips.shape, bf16),
            pltpu.VMEM(local_clips.shape, bf16),
            pltpu.SemaphoreType.DMA((2,)),
        ],
        unit // 8,
        far=True,
    )
    table = pltpu.VMEM((dp_total * rows, channels), f32)
    half = (frames // 2, height, flat, channels)
    mine = call(first_body, blocks + (shifted, base), [(half, bf16)] * 2, [table], unit)
    other = [lax.ppermute(part, "section", [(0, 1), (1, 0)]) for part in mine]
    slope, moved = call(
        between_body, (*mine, upstream), [(field, f32), (met, bf16)], [], unit // 8
    )
    slope, moved, other = lax.optimization_barrier((slope, moved, other))
    (shares,) = call(
        functools.partial(second_body, width),
        (ready, slope, moved, *other, upstream),
        [((4, 4, rows, channels), bf16)],
        [pltpu.VMEM(turned, bf16), pltpu.VMEM(met, bf16)],
        unit,
    )
    (produced,) = call(
        third_body,
        blocks + (*mine, *other),
        [(local_clips.shape, bf16)],
        [table, pltpu.VMEM(padded, bf16)],
        unit,
    )

    def added(*terms):
        return summed([term.astype(f32) for term in terms])

    received = [traded(shares[step], False, step) for step in (1, 2, 3)]
    received, produced = lax.optimization_barrier((received, produced))
    line_sum = added(shares[0, 1:], *[block[1:] for block in received]).astype(bf16)
    own_sum = added(shares[0, 0], *[block[0] for block in received])
    total = added(own_sum, *[traded(line_sum[step - 1], True, step) for step in (3, 2, 1)])
    return (produced[None, :, None], total[None])


def solution(mesh):
    dp_total = mesh.shape["dp"]
    paired = mesh.shape["section"] == 2 and dp_total == 16
    placed = (
        P(None, "dp", None, None, None, None),
        P(None, "dp", None, None, None, None),
        P("section", "dp", None),
    )
    return jax.shard_map(
        paired_sections if paired else many_sections,
        mesh=mesh,
        in_specs=placed,
        out_specs=(P("section", None, "dp", None, None, None, None), P("section", "dp", None)),
        check_vma=False,
    )
```

profile of v0, /device:TPU:0, one launch (start us, length us, event | category | flops | bytes accessed | tf_op | source)
XLA Modules:
  0.0 44.9 jit_solution(2075701567758919068)
XLA Ops:
  0.6 5.1 %collective-permute-start.2 = (bf16[216,128]{1,0:T(8,128)(2,1)}, bf16[216,128]{1,0:T(8,128)(2,1)S(1)}, u32[]{:S(2)}, u32[]{:S(2)}) collective-permute-start(bf16[216,128]{1,0:T(8,128)(2,1)} %bitcast.46), channel_id=1, source_target_pairs={{0,12},{1,13},{2,14},{3,15},{4,8},{5,9},{6,10},{7,11},{8,4},{9,5},... | collective-permute-start | bytes 165896 | tf_op jit(solution)/shard_map/ppermute | solution.py:470
  5.7 0.0 collective-permute-start.1
  5.7 0.6 %collective-permute-start = (bf16[216,128]{1,0:T(8,128)(2,1)}, bf16[216,128]{1,0:T(8,128)(2,1)S(1)}, u32[]{:S(2)}, u32[]{:S(2)}) collective-permute-start(bf16[216,128]{1,0:T(8,128)(2,1)} %bitcast.48), channel_id=1, source_target_pairs={{0,4},{1,5},{2,6},{3,7},{4,0},{5,1},{6,2},{7,3},{8,12},{9,13},{10,... | collective-permute-start | bytes 165896 | tf_op jit(solution)/shard_map/ppermute | solution.py:470
  6.4 0.0 copy-start.2
  6.4 0.8 %copy-done.2 = bf16[1,216,128]{2,1,0:T(8,128)(2,1)S(1)} copy-done((bf16[1,216,128]{2,1,0:T(8,128)(2,1)S(1)}, bf16[1,216,128]{2,1,0:T(8,128)(2,1)}, u32[]{:S(2)}) %copy-start.2) | copy-done | bytes 55320
  7.2 0.9 %collective-permute-done.2 = bf16[216,128]{1,0:T(8,128)(2,1)S(1)} collective-permute-done((bf16[216,128]{1,0:T(8,128)(2,1)}, bf16[216,128]{1,0:T(8,128)(2,1)S(1)}, u32[]{:S(2)}, u32[]{:S(2)}) %collective-permute-start.2) | collective-permute-done | bytes 55328 | tf_op jit(solution)/shard_map/ppermute | solution.py:470
  8.1 2.9 %collective-permute-done.1 = bf16[216,128]{1,0:T(8,128)(2,1)S(1)} collective-permute-done((bf16[216,128]{1,0:T(8,128)(2,1)}, bf16[216,128]{1,0:T(8,128)(2,1)S(1)}, u32[]{:S(2)}, u32[]{:S(2)}) %collective-permute-start.1) | collective-permute-done | bytes 55328 | tf_op jit(solution)/shard_map/ppermute | solution.py:470
  11.0 0.0 collective-permute-done
  11.0 4.2 %collective-permute-start.5 = (bf16[4,216,128]{2,1,0:T(8,128)(2,1)S(1)}, bf16[4,216,128]{2,1,0:T(8,128)(2,1)S(1)}, u32[]{:S(2)}, u32[]{:S(2)}) collective-permute-start(bf16[4,216,128]{2,1,0:T(8,128)(2,1)S(1)} %pad_maximum_fusion.refs_0_), channel_id=1, source_target_pairs={{0,3},{1,2},{2,1},{3,0},{4,7},{5,6},{6,5},{7,4},{8,11},{9,10},{10,... | collective-permute-start | bytes 663560 | tf_op jit(solution)/shard_map/ppermute | solution.py:470
  15.2 0.2 collective-permute-start.4
  15.4 0.4 collective-permute-start.3
  15.9 0.0 copy-start
  15.9 1.0 %copy-done = bf16[8,1,4,8,8,128]{5,4,3,2,1,0:T(8,128)(2,1)S(1)} copy-done((bf16[8,1,4,8,8,128]{5,4,3,2,1,0:T(8,128)(2,1)S(1)}, bf16[8,1,4,8,8,128]{5,4,3,2,1,0:T(8,128)(2,1)}, u32[]{:S(2)}) %copy-start) | copy-done | bytes 524312
  16.9 0.0 copy-start.1
  16.9 1.0 %copy-done.1 = bf16[8,1,4,8,8,128]{5,4,3,2,1,0:T(8,128)(2,1)S(1)} copy-done((bf16[8,1,4,8,8,128]{5,4,3,2,1,0:T(8,128)(2,1)S(1)}, bf16[8,1,4,8,8,128]{5,4,3,2,1,0:T(8,128)(2,1)}, u32[]{:S(2)}) %copy-start.1) | copy-done | bytes 524312
  17.9 0.8 %shard_map.50 = (bf16[3,4,10,64,128]{4,3,2,1,0:T(8,128)(2,1)S(1)}, bf16[4,8,64,128]{3,2,1,0:T(8,128)(2,1)S(1)}, bf16[4,8,64,128]{3,2,1,0:T(8,128)(2,1)S(1)}, bf16[384,2048]{1,0:T(8,128)(2,1)S(1)}) custom-call(bf16[8,4,8,8,128]{4,3,2,1,0:T(8,128)(2,1)S(1)} %bitcast.43, bf16[8,4,8,8,128]{4,3,2,1,0:T(8,128)(2,1)S(1)} %bitcast.44), custom_call_target="tpu_custom_call" | custom-call | flops 226492416 | bytes 4000000 | tf_op jit(solution)/shard_map/pallas_call | solution.py:161
  18.7 0.5 %collective-permute-done.5.refs_3_ = bf16[4,216,128]{2,1,0:T(8,128)(2,1)S(1)} collective-permute-done((bf16[4,216,128]{2,1,0:T(8,128)(2,1)S(1)}, bf16[4,216,128]{2,1,0:T(8,128)(2,1)S(1)}, u32[]{:S(2)}, u32[]{:S(2)}) %collective-permute-start.5) | collective-permute-done | bytes 221216 | tf_op jit(solution)/shard_map/ppermute | solution.py:470
  19.2 2.3 %collective-permute-done.4.refs_2_ = bf16[4,216,128]{2,1,0:T(8,128)(2,1)S(1)} collective-permute-done((bf16[4,216,128]{2,1,0:T(8,128)(2,1)S(1)}, bf16[4,216,128]{2,1,0:T(8,128)(2,1)S(1)}, u32[]{:S(2)}, u32[]{:S(2)}) %collective-permute-start.4) | collective-permute-done | bytes 221216 | tf_op jit(solution)/shard_map/ppermute | solution.py:470
  21.5 0.0 collective-permute-done.3.refs_1_
  21.5 2.2 %shard_map.52 = (bf16[2,8,64,128]{3,2,1,0:T(8,128)(2,1)S(1)}, bf16[2,8,64,128]{3,2,1,0:T(8,128)(2,1)S(1)}) custom-call(bf16[4,216,128]{2,1,0:T(8,128)(2,1)S(1)} %pad_maximum_fusion.refs_0_, bf16[4,216,128]{2,1,0:T(8,128)(2,1)S(1)} %collective-permute-done.3.refs_1_, bf16[4,216,128]{2,1,0:T(8,128)(2,1)S(1)} %collective-permute-done.4.refs_2_, ...), custom_call_target="tpu_custom_call" | custom-call | flops 1811939328 | bytes 4000000 | tf_op jit(solution)/shard_map/pallas_call | solution.py:161
  23.7 0.1 collective-permute-start.6
  23.8 0.5 %collective-permute-start.7 = (bf16[2,8,64,128]{3,2,1,0:T(8,128)(2,1)S(1)}, bf16[2,8,64,128]{3,2,1,0:T(8,128)(2,1)S(1)}, u32[]{:S(2)}, u32[]{:S(2)}) collective-permute-start(bf16[2,8,64,128]{3,2,1,0:T(8,128)(2,1)S(1)} %get-tuple-element.30.mine_high.refs_5_), channel_id=1, source_target_pairs={{0,16},{16,0},{1,17},{17,1},{2,18},{18,2},{3,19},{19,3},{4,20},{20... | collective-permute-start | bytes 786440 | tf_op jit(solution)/shard_map/ppermute | solution.py:501
  24.3 0.3 shard_map.53
  24.6 0.8 %collective-permute-done.6.other_low.refs_6_ = bf16[2,8,64,128]{3,2,1,0:T(8,128)(2,1)S(1)} collective-permute-done((bf16[2,8,64,128]{3,2,1,0:T(8,128)(2,1)S(1)}, bf16[2,8,64,128]{3,2,1,0:T(8,128)(2,1)S(1)}, u32[]{:S(2)}, u32[]{:S(2)}) %collective-permute-start.6) | collective-permute-done | bytes 262176 | tf_op jit(solution)/shard_map/ppermute | solution.py:501
  25.4 0.4 collective-permute-done.7.other_high.refs_7_
  25.7 2.2 %shard_map.54 = bf16[4,4,216,128]{3,2,1,0:T(8,128)(2,1)S(1)} custom-call(bf16[384,2048]{1,0:T(8,128)(2,1)S(1)} %get-tuple-element.22.ready, f32[4,8,64,128]{3,2,1,0:T(8,128)S(1)} %get-tuple-element.34.slope, bf16[6,10,64,128]{3,2,1,0:T(8,128)(2,1)S(1)} %get-tuple-element.35.moved, bf16[2,8,64,128]{3,2,1,0:T(8,128)(2,1)S(1)} %collective-permute-done.6.other_low.refs_6_, ...), custom_call_target="tpu_custom_call" | custom-call | flops 1811939328 | bytes 4000000 | tf_op jit(solution)/shard_map/pallas_call | solution.py:161
  28.0 2.2 %collective-permute-start.10 = (bf16[4,216,128]{2,1,0:T(8,128)(2,1)S(1)}, bf16[4,216,128]{2,1,0:T(8,128)(2,1)S(1)}, u32[]{:S(2)}, u32[]{:S(2)}) collective-permute-start(bf16[4,216,128]{2,1,0:T(8,128)(2,1)S(1)} %get-tuple-element.44), channel_id=1, source_target_pairs={{0,3},{1,2},{2,1},{3,0},{4,7},{5,6},{6,5},{7,4},{8,11},{9,10},{10,... | collective-permute-start | bytes 663560 | tf_op jit(solution)/shard_map/ppermute | solution.py:470
  30.1 1.4 %collective-permute-start.9 = (bf16[4,216,128]{2,1,0:T(8,128)(2,1)S(1)}, bf16[4,216,128]{2,1,0:T(8,128)(2,1)S(1)}, u32[]{:S(2)}, u32[]{:S(2)}) collective-permute-start(bf16[4,216,128]{2,1,0:T(8,128)(2,1)S(1)} %get-tuple-element.45), channel_id=1, source_target_pairs={{0,2},{1,3},{2,0},{3,1},{4,6},{5,7},{6,4},{7,5},{8,10},{9,11},{10,... | collective-permute-start | bytes 663560 | tf_op jit(solution)/shard_map/ppermute | solution.py:470
  31.6 0.0 collective-permute-start.8
  31.6 0.9 %shard_map.55 = bf16[8,4,8,8,128]{4,3,2,1,0:T(8,128)(2,1)} custom-call(bf16[4,216,128]{2,1,0:T(8,128)(2,1)S(1)} %pad_maximum_fusion.refs_0_, bf16[4,216,128]{2,1,0:T(8,128)(2,1)S(1)} %collective-permute-done.3.refs_1_, bf16[4,216,128]{2,1,0:T(8,128)(2,1)S(1)} %collective-permute-done.4.refs_2_, bf16[4,216,128]{2,1,0:T(8,128)(2,1)S(1)} %collective-permute-done.5.refs_3_, ...), custom_call_target="tpu_custom_call" | custom-call | flops 1811939328 | bytes 4000000 | tf_op jit(solution)/shard_map/pallas_call | solution.py:161
  32.4 2.5 %collective-permute-done.10 = bf16[4,216,128]{2,1,0:T(8,128)(2,1)S(1)} collective-permute-done((bf16[4,216,128]{2,1,0:T(8,128)(2,1)S(1)}, bf16[4,216,128]{2,1,0:T(8,128)(2,1)S(1)}, u32[]{:S(2)}, u32[]{:S(2)}) %collective-permute-start.10) | collective-permute-done | bytes 221216 | tf_op jit(solution)/shard_map/ppermute | solution.py:470
  35.0 2.3 %collective-permute-done.9 = bf16[4,216,128]{2,1,0:T(8,128)(2,1)S(1)} collective-permute-done((bf16[4,216,128]{2,1,0:T(8,128)(2,1)S(1)}, bf16[4,216,128]{2,1,0:T(8,128)(2,1)S(1)}, u32[]{:S(2)}, u32[]{:S(2)}) %collective-permute-start.9) | collective-permute-done | bytes 221216 | tf_op jit(solution)/shard_map/ppermute | solution.py:470
  37.2 0.3 collective-permute-done.8
  37.5 0.1 fusion.2
  37.6 1.1 %collective-permute-start.11 = (bf16[216,128]{1,0:T(8,128)(2,1)S(1)}, bf16[216,128]{1,0:T(8,128)(2,1)S(1)}, u32[]{:S(2)}, u32[]{:S(2)}) collective-permute-start(bf16[216,128]{1,0:T(8,128)(2,1)S(1)} %get-tuple-element.47), channel_id=1, source_target_pairs={{0,12},{1,13},{2,14},{3,15},{4,8},{5,9},{6,10},{7,11},{8,4},{9,5},... | collective-permute-start | bytes 165896 | tf_op jit(solution)/shard_map/ppermute | solution.py:470
  38.7 0.4 collective-permute-start.13
  39.2 2.9 %collective-permute-start.12 = (bf16[216,128]{1,0:T(8,128)(2,1)S(1)}, bf16[216,128]{1,0:T(8,128)(2,1)S(1)}, u32[]{:S(2)}, u32[]{:S(2)}) collective-permute-start(bf16[216,128]{1,0:T(8,128)(2,1)S(1)} %get-tuple-element.49), channel_id=1, source_target_pairs={{0,8},{1,9},{2,10},{3,11},{4,12},{5,13},{6,14},{7,15},{8,0},{9,1},... | collective-permute-start | bytes 165896 | tf_op jit(solution)/shard_map/ppermute | solution.py:470
  42.1 1.6 %collective-permute-done.11 = bf16[216,128]{1,0:T(8,128)(2,1)S(1)} collective-permute-done((bf16[216,128]{1,0:T(8,128)(2,1)S(1)}, bf16[216,128]{1,0:T(8,128)(2,1)S(1)}, u32[]{:S(2)}, u32[]{:S(2)}) %collective-permute-start.11) | collective-permute-done | bytes 55328 | tf_op jit(solution)/shard_map/ppermute | solution.py:470
  43.6 0.0 collective-permute-done.13
  43.6 0.6 %collective-permute-done.12 = bf16[216,128]{1,0:T(8,128)(2,1)S(1)} collective-permute-done((bf16[216,128]{1,0:T(8,128)(2,1)S(1)}, bf16[216,128]{1,0:T(8,128)(2,1)S(1)}, u32[]{:S(2)}, u32[]{:S(2)}) %collective-permute-start.12) | collective-permute-done | bytes 55328 | tf_op jit(solution)/shard_map/ppermute | solution.py:470
  44.2 0.7 %fusion.6 = f32[1,216,128]{2,1,0:T(8,128)} fusion(bf16[216,128]{1,0:T(8,128)(2,1)S(1)} %collective-permute-done.13, bf16[216,128]{1,0:T(8,128)(2,1)S(1)} %collective-permute-done.12, bf16[216,128]{1,0:T(8,128)(2,1)S(1)} %collective-permute-done.11, bf16[4,4,216,128]{3,2,1,0:T(8,128)(2,1)S(1)} %shard_map.54, ...), kind=kLoop, calls=%fused_computation.13 | loop fusion | flops 359424 | bytes 497664 | tf_op jit(solution)/shard_map/broadcast_in_dim | solution.py:529
  (4 shorter events, 0.1 us)
Async XLA Ops:
  0.6 7.5 %collective-permute-start.2 = (bf16[216,128]{1,0:T(8,128)(2,1)}, bf16[216,128]{1,0:T(8,128)(2,1)S(1)}, u32[]{:S(2)}, u32[]{:S(2)}) collective-permute-start(bf16[216,128]{1,0:T(8,128)(2,1)} %bitcast.46), channel_id=1, source_target_pairs={{0,12},{1,13},{2,14},{3,15},{4,8},{5,9},{6,10},{7,11},{8,4},{9,5},... | collective-permute-start | bytes 165896 | tf_op jit(solution)/shard_map/ppermute | solution.py:470
  5.7 5.3 %collective-permute-start.1 = (bf16[216,128]{1,0:T(8,128)(2,1)}, bf16[216,128]{1,0:T(8,128)(2,1)S(1)}, u32[]{:S(2)}, u32[]{:S(2)}) collective-permute-start(bf16[216,128]{1,0:T(8,128)(2,1)} %bitcast.47), channel_id=1, source_target_pairs={{0,8},{1,9},{2,10},{3,11},{4,12},{5,13},{6,14},{7,15},{8,0},{9,1},... | collective-permute-start | bytes 165896 | tf_op jit(solution)/shard_map/ppermute | solution.py:470
  5.7 5.3 %collective-permute-start = (bf16[216,128]{1,0:T(8,128)(2,1)}, bf16[216,128]{1,0:T(8,128)(2,1)S(1)}, u32[]{:S(2)}, u32[]{:S(2)}) collective-permute-start(bf16[216,128]{1,0:T(8,128)(2,1)} %bitcast.48), channel_id=1, source_target_pairs={{0,4},{1,5},{2,6},{3,7},{4,0},{5,1},{6,2},{7,3},{8,12},{9,13},{10,... | collective-permute-start | bytes 165896 | tf_op jit(solution)/shard_map/ppermute | solution.py:470
  6.4 0.8 %copy-start.2 = (bf16[1,216,128]{2,1,0:T(8,128)(2,1)S(1)}, bf16[1,216,128]{2,1,0:T(8,128)(2,1)}, u32[]{:S(2)}) copy-start(bf16[1,216,128]{2,1,0:T(8,128)(2,1)} %param.5) | copy-start | bytes 165892
  11.0 8.1 %collective-permute-start.5 = (bf16[4,216,128]{2,1,0:T(8,128)(2,1)S(1)}, bf16[4,216,128]{2,1,0:T(8,128)(2,1)S(1)}, u32[]{:S(2)}, u32[]{:S(2)}) collective-permute-start(bf16[4,216,128]{2,1,0:T(8,128)(2,1)S(1)} %pad_maximum_fusion.refs_0_), channel_id=1, source_target_pairs={{0,3},{1,2},{2,1},{3,0},{4,7},{5,6},{6,5},{7,4},{8,11},{9,10},{10,... | collective-permute-start | bytes 663560 | tf_op jit(solution)/shard_map/ppermute | solution.py:470
  15.2 6.3 %collective-permute-start.4 = (bf16[4,216,128]{2,1,0:T(8,128)(2,1)S(1)}, bf16[4,216,128]{2,1,0:T(8,128)(2,1)S(1)}, u32[]{:S(2)}, u32[]{:S(2)}) collective-permute-start(bf16[4,216,128]{2,1,0:T(8,128)(2,1)S(1)} %pad_maximum_fusion.refs_0_), channel_id=1, source_target_pairs={{0,2},{1,3},{2,0},{3,1},{4,6},{5,7},{6,4},{7,5},{8,10},{9,11},{10,... | collective-permute-start | bytes 663560 | tf_op jit(solution)/shard_map/ppermute | solution.py:470
  15.4 6.1 %collective-permute-start.3 = (bf16[4,216,128]{2,1,0:T(8,128)(2,1)S(1)}, bf16[4,216,128]{2,1,0:T(8,128)(2,1)S(1)}, u32[]{:S(2)}, u32[]{:S(2)}) collective-permute-start(bf16[4,216,128]{2,1,0:T(8,128)(2,1)S(1)} %pad_maximum_fusion.refs_0_), channel_id=1, source_target_pairs={{0,1},{1,0},{2,3},{3,2},{4,5},{5,4},{6,7},{7,6},{8,9},{9,8},{10,11... | collective-permute-start | bytes 663560 | tf_op jit(solution)/shard_map/ppermute | solution.py:470
  15.9 1.0 %copy-start = (bf16[8,1,4,8,8,128]{5,4,3,2,1,0:T(8,128)(2,1)S(1)}, bf16[8,1,4,8,8,128]{5,4,3,2,1,0:T(8,128)(2,1)}, u32[]{:S(2)}) copy-start(bf16[8,1,4,8,8,128]{5,4,3,2,1,0:T(8,128)(2,1)} %param.3) | copy-start | bytes 1572868
  16.9 1.0 %copy-start.1 = (bf16[8,1,4,8,8,128]{5,4,3,2,1,0:T(8,128)(2,1)S(1)}, bf16[8,1,4,8,8,128]{5,4,3,2,1,0:T(8,128)(2,1)}, u32[]{:S(2)}) copy-start(bf16[8,1,4,8,8,128]{5,4,3,2,1,0:T(8,128)(2,1)} %param.4) | copy-start | bytes 1572868
  23.7 1.6 %collective-permute-start.6 = (bf16[2,8,64,128]{3,2,1,0:T(8,128)(2,1)S(1)}, bf16[2,8,64,128]{3,2,1,0:T(8,128)(2,1)S(1)}, u32[]{:S(2)}, u32[]{:S(2)}) collective-permute-start(bf16[2,8,64,128]{3,2,1,0:T(8,128)(2,1)S(1)} %get-tuple-element.29.mine_low.refs_4_), channel_id=1, source_target_pairs={{0,16},{16,0},{1,17},{17,1},{2,18},{18,2},{3,19},{19,3},{4,20},{20... | collective-permute-start | bytes 786440 | tf_op jit(solution)/shard_map/ppermute | solution.py:501
  23.8 1.9 %collective-permute-start.7 = (bf16[2,8,64,128]{3,2,1,0:T(8,128)(2,1)S(1)}, bf16[2,8,64,128]{3,2,1,0:T(8,128)(2,1)S(1)}, u32[]{:S(2)}, u32[]{:S(2)}) collective-permute-start(bf16[2,8,64,128]{3,2,1,0:T(8,128)(2,1)S(1)} %get-tuple-element.30.mine_high.refs_5_), channel_id=1, source_target_pairs={{0,16},{16,0},{1,17},{17,1},{2,18},{18,2},{3,19},{19,3},{4,20},{20... | collective-permute-start | bytes 786440 | tf_op jit(solution)/shard_map/ppermute | solution.py:501
  28.0 7.0 %collective-permute-start.10 = (bf16[4,216,128]{2,1,0:T(8,128)(2,1)S(1)}, bf16[4,216,128]{2,1,0:T(8,128)(2,1)S(1)}, u32[]{:S(2)}, u32[]{:S(2)}) collective-permute-start(bf16[4,216,128]{2,1,0:T(8,128)(2,1)S(1)} %get-tuple-element.44), channel_id=1, source_target_pairs={{0,3},{1,2},{2,1},{3,0},{4,7},{5,6},{6,5},{7,4},{8,11},{9,10},{10,... | collective-permute-start | bytes 663560 | tf_op jit(solution)/shard_map/ppermute | solution.py:470
  30.1 7.1 %collective-permute-start.9 = (bf16[4,216,128]{2,1,0:T(8,128)(2,1)S(1)}, bf16[4,216,128]{2,1,0:T(8,128)(2,1)S(1)}, u32[]{:S(2)}, u32[]{:S(2)}) collective-permute-start(bf16[4,216,128]{2,1,0:T(8,128)(2,1)S(1)} %get-tuple-element.45), channel_id=1, source_target_pairs={{0,2},{1,3},{2,0},{3,1},{4,6},{5,7},{6,4},{7,5},{8,10},{9,11},{10,... | collective-permute-start | bytes 663560 | tf_op jit(solution)/shard_map/ppermute | solution.py:470
  31.6 5.9 %collective-permute-start.8 = (bf16[4,216,128]{2,1,0:T(8,128)(2,1)S(1)}, bf16[4,216,128]{2,1,0:T(8,128)(2,1)S(1)}, u32[]{:S(2)}, u32[]{:S(2)}) collective-permute-start(bf16[4,216,128]{2,1,0:T(8,128)(2,1)S(1)} %get-tuple-element.46), channel_id=1, source_target_pairs={{0,1},{1,0},{2,3},{3,2},{4,5},{5,4},{6,7},{7,6},{8,9},{9,8},{10,11... | collective-permute-start | bytes 663560 | tf_op jit(solution)/shard_map/ppermute | solution.py:470
  37.6 6.0 %collective-permute-start.11 = (bf16[216,128]{1,0:T(8,128)(2,1)S(1)}, bf16[216,128]{1,0:T(8,128)(2,1)S(1)}, u32[]{:S(2)}, u32[]{:S(2)}) collective-permute-start(bf16[216,128]{1,0:T(8,128)(2,1)S(1)} %get-tuple-element.47), channel_id=1, source_target_pairs={{0,12},{1,13},{2,14},{3,15},{4,8},{5,9},{6,10},{7,11},{8,4},{9,5},... | collective-permute-start | bytes 165896 | tf_op jit(solution)/shard_map/ppermute | solution.py:470
  38.7 4.9 %collective-permute-start.13 = (bf16[216,128]{1,0:T(8,128)(2,1)S(1)}, bf16[216,128]{1,0:T(8,128)(2,1)S(1)}, u32[]{:S(2)}, u32[]{:S(2)}) collective-permute-start(bf16[216,128]{1,0:T(8,128)(2,1)S(1)} %get-tuple-element.48), channel_id=1, source_target_pairs={{0,4},{1,5},{2,6},{3,7},{4,0},{5,1},{6,2},{7,3},{8,12},{9,13},{10,... | collective-permute-start | bytes 165896 | tf_op jit(solution)/shard_map/ppermute | solution.py:470
  39.2 5.1 %collective-permute-start.12 = (bf16[216,128]{1,0:T(8,128)(2,1)S(1)}, bf16[216,128]{1,0:T(8,128)(2,1)S(1)}, u32[]{:S(2)}, u32[]{:S(2)}) collective-permute-start(bf16[216,128]{1,0:T(8,128)(2,1)S(1)} %get-tuple-element.49), channel_id=1, source_target_pairs={{0,8},{1,9},{2,10},{3,11},{4,12},{5,13},{6,14},{7,15},{8,0},{9,1},... | collective-permute-start | bytes 165896 | tf_op jit(solution)/shard_map/ppermute | solution.py:470
where the time goes:
time: 45.7 us; the launch traced here: 44.9 us
  starting transfers between devices  19.2 us (42%)
  waiting for transfers between devices  14.9 us (33%)
  Pallas kernels  6.33 us (14%)
  local copies, waits for them, and re-layouts  2.99 us (7%)
  other arithmetic  0.83 us (2%)
  between operations  0.71 us (2%)
    ppermute x12, starting transfers between devices, traded(): return lax.ppermute(block, ('section', 'dp'), route)  18.6 us
    ppermute x12, waiting for transfers between devices, traded(): return lax.ppermute(block, ('section', 'dp'), route)  13.8 us
    pallas_call x6, Pallas kernels, call(): pl.pallas_call(body, out_shape=[jax.ShapeDtypeStruct(shape, dtype) for sh...  6.33 us
    unnamed x6, local copies, waits for them, and re-layouts  2.93 us
    ppermute x2, waiting for transfers between devices, paired_sections(): other = [lax.ppermute(part, 'section', [(0, 1), (1, 0)]) for part in mine]  1.13 us
  transfers between devices with their start and end apart: 14, of which 11 were waited for; matrix products, arithmetic and copies ran while one was open for 0% of the time, Pallas kernels for 4%

commit v1 on v0

--- a/solution.py
+++ b/solution.py
@@ -157,13 +157,14 @@
     return [pl.BlockSpec(memory_space=pltpu.VMEM)] * count
 
 
-def call(body, inputs, outputs, scratch, flops, far=False):
+def call(body, inputs, outputs, scratch, flops, far=False, aliases=None):
     return pl.pallas_call(
         body,
         out_shape=[jax.ShapeDtypeStruct(shape, dtype) for shape, dtype in outputs],
         in_specs=[pl.BlockSpec(memory_space=pl.ANY)] * len(inputs) if far else whole(len(inputs)),
         out_specs=whole(len(outputs)),
         scratch_shapes=scratch,
+        input_output_aliases=aliases or {},
         compiler_params=pltpu.CompilerParams(vmem_limit_bytes=32 * 1024 * 1024),
         cost_estimate=pl.CostEstimate(flops=flops, bytes_accessed=4_000_000, transcendentals=0),
     )(*inputs)
@@ -242,12 +243,23 @@
     return pl.ds(pl.multiple_of((index ^ (4 * far + near)) * rows, 8), rows)
 
 
-def unpack_weights(blocks, table):
-    rows = blocks[0].shape[1]
-    for second in range(4):
-        for first in range(4):
-            shard = blocks[second][first]
-            table[shard_rows(rows, first, second), :] = shard.astype(jnp.float32)
+def put_block(block, second, table):
+    for first in range(4):
+        rows = shard_rows(block.shape[1], first, second)
+        table[rows, :] = block[first].astype(jnp.float32)
+
+
+def fill_body(second, block, table_before, table):
+    put_block(block, second, table)
+
+
+def start_table_body(block, table):
+    put_block(block, 0, table)
+
+
+def last_sum_body(own, *refs):
+    *received, total = refs
+    total[...] = summed([own[...]] + [block[...].astype(jnp.float32) for block in received])
 
 
 def forward_weights(table, channels):
@@ -325,11 +337,10 @@
 
 
 def first_body(*refs):
-    blocks = refs[:4]
-    shifted, base, *results, table = refs[4:]
+    last_block, table_before, shifted, base, *results, table = refs
     frames, height, flat, channels = base.shape
     section = lax.axis_index("section")
-    unpack_weights(blocks, table)
+    put_block(last_block, 1, table)
 
     @pl.when(section == 0)
     def _():
@@ -424,8 +435,8 @@
 
 
 def third_body(*refs):
-    blocks = refs[:4]
-    mine, other, (produced, table, shifted) = refs[4:6], refs[6:8], refs[8:]
+    table, (produced, shifted) = refs[0], refs[5:]
+    mine, other = refs[1:3], refs[3:5]
     micro, frames, height, width, channels = produced.shape
     flat = micro * width
     section = lax.axis_index("section")
@@ -441,7 +452,6 @@
 
     @pl.when(section != 0)
     def _():
-        unpack_weights(blocks, table)
         zero_row = jnp.zeros((3, frames, 1, flat, channels), jnp.bfloat16)
         shifted[:, :, :1] = zero_row
         shifted[:, :, height + 1 :] = zero_row
@@ -479,7 +489,7 @@
     (shard_copy,) = call(copy_body, (shard,), [(shard.shape, bf16)], [], unit // 16)
     shard_copy, first = lax.optimization_barrier((shard_copy, first))
     line = jnp.stack([shard_copy] + first)
-    blocks = (line, *[traded(line, False, step) for step in range(1, 4)])
+    blocks = [traded(line, False, step) for step in range(1, 4)]
 
     turned = (3 * channels, frames * cells)
     shifted, base, upstream, ready = call(
@@ -495,9 +505,26 @@
         unit // 8,
         far=True,
     )
-    table = pltpu.VMEM((dp_total * rows, channels), f32)
+    full = ((dp_total * rows, channels), f32)
+    (table,) = call(start_table_body, (line,), [full], [], unit // 100)
+    for second in (3, 2):
+        (table,) = call(
+            functools.partial(fill_body, second),
+            (blocks[second - 1], table),
+            [full],
+            [],
+            unit // 100,
+            aliases={1: 0},
+        )
     half = (frames // 2, height, flat, channels)
-    mine = call(first_body, blocks + (shifted, base), [(half, bf16)] * 2, [table], unit)
+    *mine, table = call(
+        first_body,
+        (blocks[0], table, shifted, base),
+        [(half, bf16)] * 2 + [full],
+        [],
+        unit,
+        aliases={1: 2},
+    )
     other = [lax.ppermute(part, "section", [(0, 1), (1, 0)]) for part in mine]
     slope, moved = call(
         between_body, (*mine, upstream), [(field, f32), (met, bf16)], [], unit // 8
@@ -512,9 +539,9 @@
     )
     (produced,) = call(
         third_body,
-        blocks + (*mine, *other),
+        (table, *mine, *other),
         [(local_clips.shape, bf16)],
-        [table, pltpu.VMEM(padded, bf16)],
+        [pltpu.VMEM(padded, bf16)],
         unit,
     )
 
@@ -525,7 +552,8 @@
     received, produced = lax.optimization_barrier((received, produced))
     line_sum = added(shares[0, 1:], *[block[1:] for block in received]).astype(bf16)
     own_sum = added(shares[0, 0], *[block[0] for block in received])
-    total = added(own_sum, *[traded(line_sum[step - 1], True, step) for step in (3, 2, 1)])
+    arrived = [traded(line_sum[step - 1], True, step) for step in range(1, 4)]
+    (total,) = call(last_sum_body, (own_sum, *arrived), [(own_sum.shape, f32)], [], unit // 100)
     return (produced[None, :, None], total[None])
 
 

time: 45.7 us -> 45.7 us (level)
  Pallas kernels: 6.33 us -> 7 us
  other arithmetic: 0.83 us -> 0.16 us
  waiting for transfers between devices: 14.9 us -> 15.4 us
    broadcast_in_dim x1 -> x0, other arithmetic: 0.7 us -> none  [paired_sections(): return (produced[None, :, None], total[None])]
    pallas_call x6 -> x10, Pallas kernels: 6.33 us -> 7 us  [call(): pl.pallas_call(body, out_shape=[jax.ShapeDtypeStruct(shape, dtype) for sh...]
    ppermute x12, waiting for transfers between devices: 13.8 us -> 14.2 us  [traded(): return lax.ppermute(block, ('section', 'dp'), route)]
where the time goes in v1:
time: 45.7 us; the launch traced here: 45.4 us
  starting transfers between devices  19.1 us (42%)
  waiting for transfers between devices  15.4 us (34%)
  Pallas kernels  7 us (15%)
  local copies, waits for them, and re-layouts  2.99 us (7%)
  between operations  0.74 us (2%)
    ppermute x12, starting transfers between devices, traded(): return lax.ppermute(block, ('section', 'dp'), route)  18.6 us
    ppermute x12, waiting for transfers between devices, traded(): return lax.ppermute(block, ('section', 'dp'), route)  14.2 us
    pallas_call x10, Pallas kernels, call(): pl.pallas_call(body, out_shape=[jax.ShapeDtypeStruct(shape, dtype) for sh...  7 us
    unnamed x6, local copies, waits for them, and re-layouts  2.93 us
    ppermute x2, waiting for transfers between devices, paired_sections(): other = [lax.ppermute(part, 'section', [(0, 1), (1, 0)]) for part in mine]  1.13 us
  transfers between devices with their start and end apart: 14, of which 11 were waited for; matrix products, arithmetic and copies ran while one was open for 0% of the time, Pallas kernels for 4%

profile of v1, /device:TPU:0, one launch (start us, length us, event | category | flops | bytes accessed | tf_op | source)
XLA Modules:
  0.0 45.4 jit_solution(4378560763864715546)
XLA Ops:
  0.6 5.1 %collective-permute-start.2 = (bf16[216,128]{1,0:T(8,128)(2,1)}, bf16[216,128]{1,0:T(8,128)(2,1)S(1)}, u32[]{:S(2)}, u32[]{:S(2)}) collective-permute-start(bf16[216,128]{1,0:T(8,128)(2,1)} %bitcast.45), channel_id=1, source_target_pairs={{0,12},{1,13},{2,14},{3,15},{4,8},{5,9},{6,10},{7,11},{8,4},{9,5},... | collective-permute-start | bytes 165896 | tf_op jit(solution)/shard_map/ppermute | solution.py:480
  5.7 0.0 collective-permute-start.1
  5.7 0.6 %collective-permute-start = (bf16[216,128]{1,0:T(8,128)(2,1)}, bf16[216,128]{1,0:T(8,128)(2,1)S(1)}, u32[]{:S(2)}, u32[]{:S(2)}) collective-permute-start(bf16[216,128]{1,0:T(8,128)(2,1)} %bitcast.47), channel_id=1, source_target_pairs={{0,4},{1,5},{2,6},{3,7},{4,0},{5,1},{6,2},{7,3},{8,12},{9,13},{10,... | collective-permute-start | bytes 165896 | tf_op jit(solution)/shard_map/ppermute | solution.py:480
  6.4 0.0 copy-start.2
  6.4 0.8 %copy-done.2 = bf16[1,216,128]{2,1,0:T(8,128)(2,1)S(1)} copy-done((bf16[1,216,128]{2,1,0:T(8,128)(2,1)S(1)}, bf16[1,216,128]{2,1,0:T(8,128)(2,1)}, u32[]{:S(2)}) %copy-start.2) | copy-done | bytes 55320
  7.2 0.9 %collective-permute-done.2 = bf16[216,128]{1,0:T(8,128)(2,1)S(1)} collective-permute-done((bf16[216,128]{1,0:T(8,128)(2,1)}, bf16[216,128]{1,0:T(8,128)(2,1)S(1)}, u32[]{:S(2)}, u32[]{:S(2)}) %collective-permute-start.2) | collective-permute-done | bytes 55328 | tf_op jit(solution)/shard_map/ppermute | solution.py:480
  8.1 2.9 %collective-permute-done.1 = bf16[216,128]{1,0:T(8,128)(2,1)S(1)} collective-permute-done((bf16[216,128]{1,0:T(8,128)(2,1)}, bf16[216,128]{1,0:T(8,128)(2,1)S(1)}, u32[]{:S(2)}, u32[]{:S(2)}) %collective-permute-start.1) | collective-permute-done | bytes 55328 | tf_op jit(solution)/shard_map/ppermute | solution.py:480
  11.0 0.0 collective-permute-done
  11.0 4.2 %collective-permute-start.5 = (bf16[4,216,128]{2,1,0:T(8,128)(2,1)S(1)}, bf16[4,216,128]{2,1,0:T(8,128)(2,1)S(1)}, u32[]{:S(2)}, u32[]{:S(2)}) collective-permute-start(bf16[4,216,128]{2,1,0:T(8,128)(2,1)S(1)} %pad_maximum_fusion.block), channel_id=1, source_target_pairs={{0,3},{1,2},{2,1},{3,0},{4,7},{5,6},{6,5},{7,4},{8,11},{9,10},{10,... | collective-permute-start | bytes 663560 | tf_op jit(solution)/shard_map/ppermute | solution.py:480
  15.2 0.2 collective-permute-start.4
  15.4 0.4 collective-permute-start.3
  15.9 0.0 copy-start
  15.9 1.0 %copy-done = bf16[8,1,4,8,8,128]{5,4,3,2,1,0:T(8,128)(2,1)S(1)} copy-done((bf16[8,1,4,8,8,128]{5,4,3,2,1,0:T(8,128)(2,1)S(1)}, bf16[8,1,4,8,8,128]{5,4,3,2,1,0:T(8,128)(2,1)}, u32[]{:S(2)}) %copy-start) | copy-done | bytes 524312
  16.9 0.0 copy-start.1
  16.9 1.0 %copy-done.1 = bf16[8,1,4,8,8,128]{5,4,3,2,1,0:T(8,128)(2,1)S(1)} copy-done((bf16[8,1,4,8,8,128]{5,4,3,2,1,0:T(8,128)(2,1)S(1)}, bf16[8,1,4,8,8,128]{5,4,3,2,1,0:T(8,128)(2,1)}, u32[]{:S(2)}) %copy-start.1) | copy-done | bytes 524312
  17.9 0.7 %shard_map.50 = (bf16[3,4,10,64,128]{4,3,2,1,0:T(8,128)(2,1)S(1)}, bf16[4,8,64,128]{3,2,1,0:T(8,128)(2,1)S(1)}, bf16[4,8,64,128]{3,2,1,0:T(8,128)(2,1)S(1)}, bf16[384,2048]{1,0:T(8,128)(2,1)S(1)}) custom-call(bf16[8,4,8,8,128]{4,3,2,1,0:T(8,128)(2,1)S(1)} %bitcast.42, bf16[8,4,8,8,128]{4,3,2,1,0:T(8,128)(2,1)S(1)} %bitcast.43), custom_call_target="tpu_custom_call" | custom-call | flops 226492416 | bytes 4000000 | tf_op jit(solution)/shard_map/pallas_call | solution.py:161
  18.7 0.4 collective-permute-done.5.block
  19.2 2.3 %collective-permute-done.4.block = bf16[4,216,128]{2,1,0:T(8,128)(2,1)S(1)} collective-permute-done((bf16[4,216,128]{2,1,0:T(8,128)(2,1)S(1)}, bf16[4,216,128]{2,1,0:T(8,128)(2,1)S(1)}, u32[]{:S(2)}, u32[]{:S(2)}) %collective-permute-start.4) | collective-permute-done | bytes 221216 | tf_op jit(solution)/shard_map/ppermute | solution.py:480
  21.5 0.0 collective-permute-done.3.refs_0_
  21.6 2.1 %shard_map.55 = (bf16[2,8,64,128]{3,2,1,0:T(8,128)(2,1)S(1)}, bf16[2,8,64,128]{3,2,1,0:T(8,128)(2,1)S(1)}, f32[3456,128]{1,0:T(8,128)S(1)}) custom-call(bf16[4,216,128]{2,1,0:T(8,128)(2,1)S(1)} %collective-permute-done.3.refs_0_, f32[3456,128]{1,0:T(8,128)S(1)} %shard_map.54.refs_1_, ...), custom_call_target="tpu_custom_call", output_to_operand_aliasing={{2}: (1, {})} | custom-call | flops 1811939328 | bytes 4000000 | tf_op jit(solution)/shard_map/pallas_call | solution.py:161
  23.7 0.1 collective-permute-start.6
  23.8 0.5 %collective-permute-start.7 = (bf16[2,8,64,128]{3,2,1,0:T(8,128)(2,1)S(1)}, bf16[2,8,64,128]{3,2,1,0:T(8,128)(2,1)S(1)}, u32[]{:S(2)}, u32[]{:S(2)}) collective-permute-start(bf16[2,8,64,128]{3,2,1,0:T(8,128)(2,1)S(1)} %get-tuple-element.31.mine_high.refs_2_), channel_id=1, source_target_pairs={{0,16},{16,0},{1,17},{17,1},{2,18},{18,2},{3,19},{19,3},{4,20},{20... | collective-permute-start | bytes 786440 | tf_op jit(solution)/shard_map/ppermute | solution.py:528
  24.3 0.3 shard_map.56
  24.5 0.8 %collective-permute-done.6.other_low.refs_3_ = bf16[2,8,64,128]{3,2,1,0:T(8,128)(2,1)S(1)} collective-permute-done((bf16[2,8,64,128]{3,2,1,0:T(8,128)(2,1)S(1)}, bf16[2,8,64,128]{3,2,1,0:T(8,128)(2,1)S(1)}, u32[]{:S(2)}, u32[]{:S(2)}) %collective-permute-start.6) | collective-permute-done | bytes 262176 | tf_op jit(solution)/shard_map/ppermute | solution.py:528
  25.3 0.4 collective-permute-done.7.other_high.refs_4_
  25.7 2.2 %shard_map.57 = bf16[4,4,216,128]{3,2,1,0:T(8,128)(2,1)S(1)} custom-call(bf16[384,2048]{1,0:T(8,128)(2,1)S(1)} %get-tuple-element.23.ready, f32[4,8,64,128]{3,2,1,0:T(8,128)S(1)} %get-tuple-element.35.slope, bf16[6,10,64,128]{3,2,1,0:T(8,128)(2,1)S(1)} %get-tuple-element.36.moved, bf16[2,8,64,128]{3,2,1,0:T(8,128)(2,1)S(1)} %collective-permute-done.6.other_low.refs_3_, ...), custom_call_target="tpu_custom_call" | custom-call | flops 1811939328 | bytes 4000000 | tf_op jit(solution)/shard_map/pallas_call | solution.py:161
  27.9 2.2 %collective-permute-start.10 = (bf16[4,216,128]{2,1,0:T(8,128)(2,1)S(1)}, bf16[4,216,128]{2,1,0:T(8,128)(2,1)S(1)}, u32[]{:S(2)}, u32[]{:S(2)}) collective-permute-start(bf16[4,216,128]{2,1,0:T(8,128)(2,1)S(1)} %get-tuple-element.46), channel_id=1, source_target_pairs={{0,3},{1,2},{2,1},{3,0},{4,7},{5,6},{6,5},{7,4},{8,11},{9,10},{10,... | collective-permute-start | bytes 663560 | tf_op jit(solution)/shard_map/ppermute | solution.py:480
  30.1 1.4 %collective-permute-start.9 = (bf16[4,216,128]{2,1,0:T(8,128)(2,1)S(1)}, bf16[4,216,128]{2,1,0:T(8,128)(2,1)S(1)}, u32[]{:S(2)}, u32[]{:S(2)}) collective-permute-start(bf16[4,216,128]{2,1,0:T(8,128)(2,1)S(1)} %get-tuple-element.47), channel_id=1, source_target_pairs={{0,2},{1,3},{2,0},{3,1},{4,6},{5,7},{6,4},{7,5},{8,10},{9,11},{10,... | collective-permute-start | bytes 663560 | tf_op jit(solution)/shard_map/ppermute | solution.py:480
  31.4 0.0 collective-permute-start.8
  31.5 0.9 %shard_map.58 = bf16[8,4,8,8,128]{4,3,2,1,0:T(8,128)(2,1)} custom-call(f32[3456,128]{1,0:T(8,128)S(1)} %get-tuple-element.39.refs_0_, bf16[2,8,64,128]{3,2,1,0:T(8,128)(2,1)S(1)} %get-tuple-element.30.mine_low.refs_1_, bf16[2,8,64,128]{3,2,1,0:T(8,128)(2,1)S(1)} %get-tuple-element.31.mine_high.refs_2_, ...), custom_call_target="tpu_custom_call" | custom-call | flops 1811939328 | bytes 4000000 | tf_op jit(solution)/shard_map/pallas_call | solution.py:161
  32.3 2.6 %collective-permute-done.10 = bf16[4,216,128]{2,1,0:T(8,128)(2,1)S(1)} collective-permute-done((bf16[4,216,128]{2,1,0:T(8,128)(2,1)S(1)}, bf16[4,216,128]{2,1,0:T(8,128)(2,1)S(1)}, u32[]{:S(2)}, u32[]{:S(2)}) %collective-permute-start.10) | collective-permute-done | bytes 221216 | tf_op jit(solution)/shard_map/ppermute | solution.py:480
  34.9 2.3 %collective-permute-done.9 = bf16[4,216,128]{2,1,0:T(8,128)(2,1)S(1)} collective-permute-done((bf16[4,216,128]{2,1,0:T(8,128)(2,1)S(1)}, bf16[4,216,128]{2,1,0:T(8,128)(2,1)S(1)}, u32[]{:S(2)}, u32[]{:S(2)}) %collective-permute-start.9) | collective-permute-done | bytes 221216 | tf_op jit(solution)/shard_map/ppermute | solution.py:480
  37.2 0.2 collective-permute-done.8
  37.4 0.1 fusion.2
  37.5 1.2 %collective-permute-start.13 = (bf16[216,128]{1,0:T(8,128)(2,1)S(1)}, bf16[216,128]{1,0:T(8,128)(2,1)S(1)}, u32[]{:S(2)}, u32[]{:S(2)}) collective-permute-start(bf16[216,128]{1,0:T(8,128)(2,1)S(1)} %get-tuple-element.49), channel_id=1, source_target_pairs={{0,12},{1,13},{2,14},{3,15},{4,8},{5,9},{6,10},{7,11},{8,4},{9,5},... | collective-permute-start | bytes 165896 | tf_op jit(solution)/shard_map/ppermute | solution.py:480
  38.7 0.0 collective-permute-start.12
  38.7 3.3 %collective-permute-start.11 = (bf16[216,128]{1,0:T(8,128)(2,1)S(1)}, bf16[216,128]{1,0:T(8,128)(2,1)S(1)}, u32[]{:S(2)}, u32[]{:S(2)}) collective-permute-start(bf16[216,128]{1,0:T(8,128)(2,1)S(1)} %get-tuple-element.51), channel_id=1, source_target_pairs={{0,4},{1,5},{2,6},{3,7},{4,0},{5,1},{6,2},{7,3},{8,12},{9,13},{10,... | collective-permute-start | bytes 165896 | tf_op jit(solution)/shard_map/ppermute | solution.py:480
  42.0 1.6 %collective-permute-done.13.refs_2_ = bf16[216,128]{1,0:T(8,128)(2,1)S(1)} collective-permute-done((bf16[216,128]{1,0:T(8,128)(2,1)S(1)}, bf16[216,128]{1,0:T(8,128)(2,1)S(1)}, u32[]{:S(2)}, u32[]{:S(2)}) %collective-permute-start.13) | collective-permute-done | bytes 55328 | tf_op jit(solution)/shard_map/ppermute | solution.py:480
  43.6 1.1 %collective-permute-done.12.refs_1_ = bf16[216,128]{1,0:T(8,128)(2,1)S(1)} collective-permute-done((bf16[216,128]{1,0:T(8,128)(2,1)S(1)}, bf16[216,128]{1,0:T(8,128)(2,1)S(1)}, u32[]{:S(2)}, u32[]{:S(2)}) %collective-permute-start.12) | collective-permute-done | bytes 55328 | tf_op jit(solution)/shard_map/ppermute | solution.py:480
  44.7 0.0 collective-permute-done.11.refs_0_
  44.7 0.7 %shard_map.59 = f32[216,128]{1,0:T(8,128)} custom-call(f32[216,128]{1,0:T(8,128)S(1)} %convert_add_fusion.1.own, bf16[216,128]{1,0:T(8,128)(2,1)S(1)} %collective-permute-done.11.refs_0_, bf16[216,128]{1,0:T(8,128)(2,1)S(1)} %collective-permute-done.12.refs_1_, bf16[216,128]{1,0:T(8,128)(2,1)S(1)} %collective-permute-done.13.refs_2_), custom_call_target="tpu_custom_call" | custom-call | flops 18119392 | bytes 4000000 | tf_op jit(solution)/shard_map/pallas_call | solution.py:161
  (8 shorter events, 0.2 us)
Async XLA Ops:
  0.6 7.5 %collective-permute-start.2 = (bf16[216,128]{1,0:T(8,128)(2,1)}, bf16[216,128]{1,0:T(8,128)(2,1)S(1)}, u32[]{:S(2)}, u32[]{:S(2)}) collective-permute-start(bf16[216,128]{1,0:T(8,128)(2,1)} %bitcast.45), channel_id=1, source_target_pairs={{0,12},{1,13},{2,14},{3,15},{4,8},{5,9},{6,10},{7,11},{8,4},{9,5},... | collective-permute-start | bytes 165896 | tf_op jit(solution)/shard_map/ppermute | solution.py:480
  5.7 5.3 %collective-permute-start.1 = (bf16[216,128]{1,0:T(8,128)(2,1)}, bf16[216,128]{1,0:T(8,128)(2,1)S(1)}, u32[]{:S(2)}, u32[]{:S(2)}) collective-permute-start(bf16[216,128]{1,0:T(8,128)(2,1)} %bitcast.46), channel_id=1, source_target_pairs={{0,8},{1,9},{2,10},{3,11},{4,12},{5,13},{6,14},{7,15},{8,0},{9,1},... | collective-permute-start | bytes 165896 | tf_op jit(solution)/shard_map/ppermute | solution.py:480
  5.7 5.3 %collective-permute-start = (bf16[216,128]{1,0:T(8,128)(2,1)}, bf16[216,128]{1,0:T(8,128)(2,1)S(1)}, u32[]{:S(2)}, u32[]{:S(2)}) collective-permute-start(bf16[216,128]{1,0:T(8,128)(2,1)} %bitcast.47), channel_id=1, source_target_pairs={{0,4},{1,5},{2,6},{3,7},{4,0},{5,1},{6,2},{7,3},{8,12},{9,13},{10,... | collective-permute-start | bytes 165896 | tf_op jit(solution)/shard_map/ppermute | solution.py:480
  6.4 0.8 %copy-start.2 = (bf16[1,216,128]{2,1,0:T(8,128)(2,1)S(1)}, bf16[1,216,128]{2,1,0:T(8,128)(2,1)}, u32[]{:S(2)}) copy-start(bf16[1,216,128]{2,1,0:T(8,128)(2,1)} %param.5) | copy-start | bytes 165892
  11.0 8.1 %collective-permute-start.5 = (bf16[4,216,128]{2,1,0:T(8,128)(2,1)S(1)}, bf16[4,216,128]{2,1,0:T(8,128)(2,1)S(1)}, u32[]{:S(2)}, u32[]{:S(2)}) collective-permute-start(bf16[4,216,128]{2,1,0:T(8,128)(2,1)S(1)} %pad_maximum_fusion.block), channel_id=1, source_target_pairs={{0,3},{1,2},{2,1},{3,0},{4,7},{5,6},{6,5},{7,4},{8,11},{9,10},{10,... | collective-permute-start | bytes 663560 | tf_op jit(solution)/shard_map/ppermute | solution.py:480
  15.2 6.3 %collective-permute-start.4 = (bf16[4,216,128]{2,1,0:T(8,128)(2,1)S(1)}, bf16[4,216,128]{2,1,0:T(8,128)(2,1)S(1)}, u32[]{:S(2)}, u32[]{:S(2)}) collective-permute-start(bf16[4,216,128]{2,1,0:T(8,128)(2,1)S(1)} %pad_maximum_fusion.block), channel_id=1, source_target_pairs={{0,2},{1,3},{2,0},{3,1},{4,6},{5,7},{6,4},{7,5},{8,10},{9,11},{10,... | collective-permute-start | bytes 663560 | tf_op jit(solution)/shard_map/ppermute | solution.py:480
  15.4 6.1 %collective-permute-start.3 = (bf16[4,216,128]{2,1,0:T(8,128)(2,1)S(1)}, bf16[4,216,128]{2,1,0:T(8,128)(2,1)S(1)}, u32[]{:S(2)}, u32[]{:S(2)}) collective-permute-start(bf16[4,216,128]{2,1,0:T(8,128)(2,1)S(1)} %pad_maximum_fusion.block), channel_id=1, source_target_pairs={{0,1},{1,0},{2,3},{3,2},{4,5},{5,4},{6,7},{7,6},{8,9},{9,8},{10,11... | collective-permute-start | bytes 663560 | tf_op jit(solution)/shard_map/ppermute | solution.py:480
  15.9 1.0 %copy-start = (bf16[8,1,4,8,8,128]{5,4,3,2,1,0:T(8,128)(2,1)S(1)}, bf16[8,1,4,8,8,128]{5,4,3,2,1,0:T(8,128)(2,1)}, u32[]{:S(2)}) copy-start(bf16[8,1,4,8,8,128]{5,4,3,2,1,0:T(8,128)(2,1)} %param.3) | copy-start | bytes 1572868
  16.9 1.0 %copy-start.1 = (bf16[8,1,4,8,8,128]{5,4,3,2,1,0:T(8,128)(2,1)S(1)}, bf16[8,1,4,8,8,128]{5,4,3,2,1,0:T(8,128)(2,1)}, u32[]{:S(2)}) copy-start(bf16[8,1,4,8,8,128]{5,4,3,2,1,0:T(8,128)(2,1)} %param.4) | copy-start | bytes 1572868
  23.7 1.6 %collective-permute-start.6 = (bf16[2,8,64,128]{3,2,1,0:T(8,128)(2,1)S(1)}, bf16[2,8,64,128]{3,2,1,0:T(8,128)(2,1)S(1)}, u32[]{:S(2)}, u32[]{:S(2)}) collective-permute-start(bf16[2,8,64,128]{3,2,1,0:T(8,128)(2,1)S(1)} %get-tuple-element.30.mine_low.refs_1_), channel_id=1, source_target_pairs={{0,16},{16,0},{1,17},{17,1},{2,18},{18,2},{3,19},{19,3},{4,20},{20... | collective-permute-start | bytes 786440 | tf_op jit(solution)/shard_map/ppermute | solution.py:528
  23.8 1.9 %collective-permute-start.7 = (bf16[2,8,64,128]{3,2,1,0:T(8,128)(2,1)S(1)}, bf16[2,8,64,128]{3,2,1,0:T(8,128)(2,1)S(1)}, u32[]{:S(2)}, u32[]{:S(2)}) collective-permute-start(bf16[2,8,64,128]{3,2,1,0:T(8,128)(2,1)S(1)} %get-tuple-element.31.mine_high.refs_2_), channel_id=1, source_target_pairs={{0,16},{16,0},{1,17},{17,1},{2,18},{18,2},{3,19},{19,3},{4,20},{20... | collective-permute-start | bytes 786440 | tf_op jit(solution)/shard_map/ppermute | solution.py:528
  27.9 7.0 %collective-permute-start.10 = (bf16[4,216,128]{2,1,0:T(8,128)(2,1)S(1)}, bf16[4,216,128]{2,1,0:T(8,128)(2,1)S(1)}, u32[]{:S(2)}, u32[]{:S(2)}) collective-permute-start(bf16[4,216,128]{2,1,0:T(8,128)(2,1)S(1)} %get-tuple-element.46), channel_id=1, source_target_pairs={{0,3},{1,2},{2,1},{3,0},{4,7},{5,6},{6,5},{7,4},{8,11},{9,10},{10,... | collective-permute-start | bytes 663560 | tf_op jit(solution)/shard_map/ppermute | solution.py:480
  30.1 7.1 %collective-permute-start.9 = (bf16[4,216,128]{2,1,0:T(8,128)(2,1)S(1)}, bf16[4,216,128]{2,1,0:T(8,128)(2,1)S(1)}, u32[]{:S(2)}, u32[]{:S(2)}) collective-permute-start(bf16[4,216,128]{2,1,0:T(8,128)(2,1)S(1)} %get-tuple-element.47), channel_id=1, source_target_pairs={{0,2},{1,3},{2,0},{3,1},{4,6},{5,7},{6,4},{7,5},{8,10},{9,11},{10,... | collective-permute-start | bytes 663560 | tf_op jit(solution)/shard_map/ppermute | solution.py:480
  31.4 5.9 %collective-permute-start.8 = (bf16[4,216,128]{2,1,0:T(8,128)(2,1)S(1)}, bf16[4,216,128]{2,1,0:T(8,128)(2,1)S(1)}, u32[]{:S(2)}, u32[]{:S(2)}) collective-permute-start(bf16[4,216,128]{2,1,0:T(8,128)(2,1)S(1)} %get-tuple-element.48), channel_id=1, source_target_pairs={{0,1},{1,0},{2,3},{3,2},{4,5},{5,4},{6,7},{7,6},{8,9},{9,8},{10,11... | collective-permute-start | bytes 663560 | tf_op jit(solution)/shard_map/ppermute | solution.py:480
  37.5 6.1 %collective-permute-start.13 = (bf16[216,128]{1,0:T(8,128)(2,1)S(1)}, bf16[216,128]{1,0:T(8,128)(2,1)S(1)}, u32[]{:S(2)}, u32[]{:S(2)}) collective-permute-start(bf16[216,128]{1,0:T(8,128)(2,1)S(1)} %get-tuple-element.49), channel_id=1, source_target_pairs={{0,12},{1,13},{2,14},{3,15},{4,8},{5,9},{6,10},{7,11},{8,4},{9,5},... | collective-permute-start | bytes 165896 | tf_op jit(solution)/shard_map/ppermute | solution.py:480
  38.7 6.0 %collective-permute-start.12 = (bf16[216,128]{1,0:T(8,128)(2,1)S(1)}, bf16[216,128]{1,0:T(8,128)(2,1)S(1)}, u32[]{:S(2)}, u32[]{:S(2)}) collective-permute-start(bf16[216,128]{1,0:T(8,128)(2,1)S(1)} %get-tuple-element.50), channel_id=1, source_target_pairs={{0,8},{1,9},{2,10},{3,11},{4,12},{5,13},{6,14},{7,15},{8,0},{9,1},... | collective-permute-start | bytes 165896 | tf_op jit(solution)/shard_map/ppermute | solution.py:480
  38.7 6.0 %collective-permute-start.11 = (bf16[216,128]{1,0:T(8,128)(2,1)S(1)}, bf16[216,128]{1,0:T(8,128)(2,1)S(1)}, u32[]{:S(2)}, u32[]{:S(2)}) collective-permute-start(bf16[216,128]{1,0:T(8,128)(2,1)S(1)} %get-tuple-element.51), channel_id=1, source_target_pairs={{0,4},{1,5},{2,6},{3,7},{4,0},{5,1},{6,2},{7,3},{8,12},{9,13},{10,... | collective-permute-start | bytes 165896 | tf_op jit(solution)/shard_map/ppermute | solution.py:480

commit v2 on v0

--- a/solution.py
+++ b/solution.py
@@ -165,7 +165,7 @@
         out_specs=whole(len(outputs)),
         scratch_shapes=scratch,
         compiler_params=pltpu.CompilerParams(vmem_limit_bytes=32 * 1024 * 1024),
-        cost_estimate=pl.CostEstimate(flops=flops, bytes_accessed=4_000_000, transcendentals=0),
+        cost_estimate=pl.CostEstimate(flops=flops, bytes_accessed=flops // 450, transcendentals=0),
     )(*inputs)
 
 
@@ -300,66 +300,115 @@
     ]
 
 
-def backward_product(shifted, weights, frames, height):
-    channels = shifted.shape[-1]
-    cells = height * shifted.shape[-2]
-    first, second, third, first_two, all_three = weights
-    plan = (
-        (2, frames - 2, ((first, -2), (second, -1), (third, 0))),
-        (1, 1, ((third, 0), (first_two, -1))),
-        (0, 1, ((all_three, 0),)),
-    )
-    reaching = [[] for _ in range(frames)]
-    for start, count, terms in plan:
-        part = lax.dot_general(
-            row_patches(shifted, start, count, height),
-            jnp.concatenate([weight for weight, _ in terms], axis=0),
-            (((1,), (1,)), ((), ())),
-            preferred_element_type=jnp.float32,
-        )
-        for t in range(start, start + count):
-            rows = slice((t - start) * cells, (t - start + 1) * cells)
-            for column, (_, step) in enumerate(terms):
-                reaching[t + step].append(part[rows, column * channels : (column + 1) * channels])
-    return [summed(terms) for terms in reaching]
-
-
-def first_body(*refs):
-    blocks = refs[:4]
-    shifted, base, *results, table = refs[4:]
+def column(part, k, channels):
+    return part[:, k * channels : (k + 1) * channels]
+
+
+def against(patches, weights):
+    return lax.dot_general(
+        patches,
+        jnp.concatenate(weights, axis=0),
+        (((1,), (1,)), ((), ())),
+        preferred_element_type=jnp.float32,
+    )
+
+
+def first_half_body(*refs):
+    blocks, (shifted, base, result, table, carried) = refs[:4], refs[4:]
     frames, height, flat, channels = base.shape
     section = lax.axis_index("section")
     unpack_weights(blocks, table)
 
     @pl.when(section == 0)
     def _():
-        branch = forward_product(shifted, forward_weights(table, channels), frames, height)
+        weights = forward_weights(table, channels)
+        part = jnp.dot(
+            row_patches(shifted, 0, 1, height), weights, preferred_element_type=jnp.float32
+        )
+        taps = [column(part, k, channels) for k in range(3)]
+        last = jnp.dot(
+            row_patches(shifted, 1, 1, height),
+            weights[:, 2 * channels :],
+            preferred_element_type=jnp.float32,
+        )
+        carried[...] = taps[0]
+        for t, branch in enumerate((taps[0] + taps[1] + taps[2], taps[0] + taps[1] + last)):
+            total = base[t].astype(jnp.float32) + branch.reshape(height, flat, channels)
+            result[t] = total.astype(jnp.bfloat16)
+
+    @pl.when(section != 0)
+    def _():
+        _, second, third, _, _ = backward_weights(table, channels)
+        part = against(row_patches(shifted, 3, 1, height), [third, second])
+        own = against(row_patches(shifted, 2, 1, height), [third])
+        for t, branch in enumerate((own + column(part, 1, channels), column(part, 0, channels))):
+            result[t] = branch.reshape(height, flat, channels).astype(jnp.bfloat16)
+
+
+def second_half_body(table, carried, shifted, base, result):
+    frames, height, flat, channels = base.shape
+    section = lax.axis_index("section")
+
+    @pl.when(section == 0)
+    def _():
+        weights = forward_weights(table, channels)
+        parts = []
+        for t, taps in ((1, slice(0, 2)), (2, slice(1, 3)), (3, slice(2, 3))):
+            columns = weights[:, taps.start * channels : taps.stop * channels]
+            patches = row_patches(shifted, t, 1, height)
+            parts.append(jnp.dot(patches, columns, preferred_element_type=jnp.float32))
+        third = carried[...] + column(parts[0], 1, channels) + column(parts[1], 1, channels)
+        fourth = column(parts[0], 0, channels) + column(parts[1], 0, channels) + parts[2]
+        for t, branch in enumerate((third, fourth)):
+            total = base[2 + t].astype(jnp.float32) + branch.reshape(height, flat, channels)
+            result[t] = total.astype(jnp.bfloat16)
+
+    @pl.when(section != 0)
+    def _():
+        first, second, third, first_two, all_three = backward_weights(table, channels)
+        parts = [
+            against(row_patches(shifted, t, 1, height), weights)
+            for t, weights in (
+                (3, [first]),
+                (2, [second, first]),
+                (1, [third, first_two]),
+                (0, [all_three]),
+            )
+        ]
+        early = column(parts[1], 1, channels) + column(parts[2], 1, channels) + parts[3]
+        later = parts[0] + column(parts[1], 0, channels) + column(parts[2], 0, channels)
+        for t, branch in enumerate((early, later)):
+            result[t] = branch.reshape(height, flat, channels).astype(jnp.bfloat16)
+
+
+def between_body(width, mine_low, mine_high, other_first, upstream, slope, grads, turned):
+    frames = upstream.shape[0]
+    section = lax.axis_index("section")
+
+    @pl.when(section == 0)
+    def _():
         for t in range(frames):
-            total = base[t].astype(jnp.float32) + branch[t].reshape(height, flat, channels)
-            frame_of(results, t)[...] = total.astype(jnp.bfloat16)
+            here = slope_of(frame_of((mine_low, mine_high), t)[...].astype(jnp.float32))
+            if t >= frames - 2:
+                column_grad = other_first[t - 2].astype(jnp.float32)
+                here = upstream[t].astype(jnp.float32) + here * column_grad
+            slope[t] = here
 
     @pl.when(section != 0)
-    def _():
-        branch = backward_product(shifted, backward_weights(table, channels), frames, height)
-        for t in range(frames):
-            frame_of(results, t)[...] = branch[t].reshape(height, flat, channels).astype(jnp.bfloat16)
-
-
-def between_body(mine_low, mine_high, upstream, slope, grads):
-    frames = upstream.shape[0]
-
-    @pl.when(lax.axis_index("section") == 0)
-    def _():
-        for t in range(frames):
-            slope[t] = slope_of(frame_of((mine_low, mine_high), t)[...].astype(jnp.float32))
-
-    @pl.when(lax.axis_index("section") != 0)
     def _():
         pad_rows(grads)
         place_grads(grads, [upstream[t].astype(jnp.float32) for t in range(frames)])
-
-
-def second_body(width, ready, slope, moved, other_low, other_high, upstream, *refs):
+        for t in range(2):
+            turn_squashed(turned, t, other_first[t], width)
+
+
+def turn_squashed(turned, t, field, width):
+    squashed = silu_of(field.astype(jnp.float32)).astype(jnp.bfloat16)
+    for k, piece in enumerate(column_shifts(squashed.astype(jnp.float32), width)):
+        turn_into(turned, k, t, piece)
+
+
+def second_body(width, ready, slope, moved, turned_first, other_later, upstream, *refs):
     shares, turned, grads = refs
     frames, height, flat, channels = upstream.shape
     rows = shares.shape[2]
@@ -408,24 +457,22 @@
     def _():
         pad_rows(grads)
         values = [
-            upstream[t].astype(jnp.float32) + slope[t] * frame_of((other_low, other_high), t)[...].astype(jnp.float32)
-            for t in range(frames)
-        ]
+            upstream[t].astype(jnp.float32) + slope[t] * other_later[t].astype(jnp.float32)
+            for t in range(2)
+        ] + [slope[t] for t in range(2, frames)]
         place_grads(grads, [value.astype(jnp.bfloat16).astype(jnp.float32) for value in values])
-        product(ready, grads)
+        product(ready[...], grads)
 
     @pl.when(section != 0)
     def _():
-        for t in range(frames):
-            squashed = silu_of(frame_of((other_low, other_high), t)[...].astype(jnp.float32)).astype(jnp.bfloat16)
-            for k, piece in enumerate(column_shifts(squashed.astype(jnp.float32), width)):
-                turn_into(turned, k, t, piece)
-        product(turned, moved)
+        for t in range(2, frames):
+            turn_squashed(turned, t - 2, other_later[t - 2], width)
+        product(jnp.concatenate([turned_first[...], turned[...]], axis=1), moved)
 
 
 def third_body(*refs):
-    blocks = refs[:4]
-    mine, other, (produced, table, shifted) = refs[4:6], refs[6:8], refs[8:]
+    table, (produced, shifted) = refs[0], refs[5:]
+    mine, other = refs[1:3], refs[3:5]
     micro, frames, height, width, channels = produced.shape
     flat = micro * width
     section = lax.axis_index("section")
@@ -441,7 +488,6 @@
 
     @pl.when(section != 0)
     def _():
-        unpack_weights(blocks, table)
         zero_row = jnp.zeros((3, frames, 1, flat, channels), jnp.bfloat16)
         shifted[:, :, :1] = zero_row
         shifted[:, :, height + 1 :] = zero_row
@@ -495,26 +541,43 @@
         unit // 8,
         far=True,
     )
-    table = pltpu.VMEM((dp_total * rows, channels), f32)
-    half = (frames // 2, height, flat, channels)
-    mine = call(first_body, blocks + (shifted, base), [(half, bf16)] * 2, [table], unit)
-    other = [lax.ppermute(part, "section", [(0, 1), (1, 0)]) for part in mine]
-    slope, moved = call(
-        between_body, (*mine, upstream), [(field, f32), (met, bf16)], [], unit // 8
-    )
-    slope, moved, other = lax.optimization_barrier((slope, moved, other))
+    half = ((frames // 2, height, flat, channels), bf16)
+    mine_first, table, carried = call(
+        first_half_body,
+        blocks + (shifted, base),
+        [half, ((dp_total * rows, channels), f32), ((cells, channels), f32)],
+        [],
+        unit // 2,
+    )
+    other_first = lax.ppermute(mine_first, "section", [(0, 1), (1, 0)])
+    (mine_later,) = call(
+        second_half_body, (table, carried, shifted, base), [half], [], unit // 2
+    )
+    other_later = lax.ppermute(mine_later, "section", [(0, 1), (1, 0)])
+    mine = (mine_first, mine_later)
+    half_turned = (3 * channels, 2 * cells)
+    slope, moved, turned_first = call(
+        functools.partial(between_body, width),
+        (*mine, other_first, upstream),
+        [(field, f32), (met, bf16), (half_turned, bf16)],
+        [],
+        unit // 1000,
+    )
+    slope, moved, turned_first, other_later = lax.optimization_barrier(
+        (slope, moved, turned_first, other_later)
+    )
     (shares,) = call(
         functools.partial(second_body, width),
-        (ready, slope, moved, *other, upstream),
+        (ready, slope, moved, turned_first, other_later, upstream),
         [((4, 4, rows, channels), bf16)],
-        [pltpu.VMEM(turned, bf16), pltpu.VMEM(met, bf16)],
+        [pltpu.VMEM(half_turned, bf16), pltpu.VMEM(met, bf16)],
         unit,
     )
     (produced,) = call(
         third_body,
-        blocks + (*mine, *other),
+        (table, *mine, other_first, other_later),
         [(local_clips.shape, bf16)],
-        [table, pltpu.VMEM(padded, bf16)],
+        [pltpu.VMEM(padded, bf16)],
         unit,
     )
 

time: 45.7 us -> 46 us (level)
    pallas_call x6 -> x7, Pallas kernels: 6.33 us -> 6.54 us  [call(): pl.pallas_call(body, out_shape=[jax.ShapeDtypeStruct(shape, dtype) for sh...]
  transfers between devices with their start and end apart: 14 -> 14, of which waited for: 11 -> 10; matrix products, arithmetic and copies ran while one was open for 0% -> 0% of each run, Pallas kernels for 4% -> 7%
where the time goes in v2:
time: 46 us; the launch traced here: 45.2 us
  starting transfers between devices  19.6 us (43%)
  waiting for transfers between devices  14.6 us (32%)
  Pallas kernels  6.54 us (14%)
  local copies, waits for them, and re-layouts  2.99 us (6%)
  other arithmetic  0.83 us (2%)
  between operations  0.72 us (2%)
    ppermute x12, starting transfers between devices, traded(): return lax.ppermute(block, ('section', 'dp'), route)  18.6 us
    ppermute x12, waiting for transfers between devices, traded(): return lax.ppermute(block, ('section', 'dp'), route)  13.8 us
    pallas_call x7, Pallas kernels, call(): pl.pallas_call(body, out_shape=[jax.ShapeDtypeStruct(shape, dtype) for sh...  6.54 us
    unnamed x6, local copies, waits for them, and re-layouts  2.93 us
  transfers between devices with their start and end apart: 14, of which 10 were waited for; matrix products, arithmetic and copies ran while one was open for 0% of the time, Pallas kernels for 7%

profile of v2, /device:TPU:0, one launch (start us, length us, event | category | flops | bytes accessed | tf_op | source)
XLA Modules:
  0.0 45.2 jit_solution(10758608558783362645)
XLA Ops:
  0.6 5.1 %collective-permute-start.2 = (bf16[216,128]{1,0:T(8,128)(2,1)}, bf16[216,128]{1,0:T(8,128)(2,1)S(1)}, u32[]{:S(2)}, u32[]{:S(2)}) collective-permute-start(bf16[216,128]{1,0:T(8,128)(2,1)} %bitcast.46), channel_id=1, source_target_pairs={{0,12},{1,13},{2,14},{3,15},{4,8},{5,9},{6,10},{7,11},{8,4},{9,5},... | collective-permute-start | bytes 165896 | tf_op jit(solution)/shard_map/ppermute | solution.py:516
  5.7 0.0 collective-permute-start.1
  5.7 0.6 %collective-permute-start = (bf16[216,128]{1,0:T(8,128)(2,1)}, bf16[216,128]{1,0:T(8,128)(2,1)S(1)}, u32[]{:S(2)}, u32[]{:S(2)}) collective-permute-start(bf16[216,128]{1,0:T(8,128)(2,1)} %bitcast.48), channel_id=1, source_target_pairs={{0,4},{1,5},{2,6},{3,7},{4,0},{5,1},{6,2},{7,3},{8,12},{9,13},{10,... | collective-permute-start | bytes 165896 | tf_op jit(solution)/shard_map/ppermute | solution.py:516
  6.4 0.0 copy-start.2
  6.4 0.8 %copy-done.2 = bf16[1,216,128]{2,1,0:T(8,128)(2,1)S(1)} copy-done((bf16[1,216,128]{2,1,0:T(8,128)(2,1)S(1)}, bf16[1,216,128]{2,1,0:T(8,128)(2,1)}, u32[]{:S(2)}) %copy-start.2) | copy-done | bytes 55320
  7.2 0.9 %collective-permute-done.2 = bf16[216,128]{1,0:T(8,128)(2,1)S(1)} collective-permute-done((bf16[216,128]{1,0:T(8,128)(2,1)}, bf16[216,128]{1,0:T(8,128)(2,1)S(1)}, u32[]{:S(2)}, u32[]{:S(2)}) %collective-permute-start.2) | collective-permute-done | bytes 55328 | tf_op jit(solution)/shard_map/ppermute | solution.py:516
  8.1 2.9 %collective-permute-done.1 = bf16[216,128]{1,0:T(8,128)(2,1)S(1)} collective-permute-done((bf16[216,128]{1,0:T(8,128)(2,1)}, bf16[216,128]{1,0:T(8,128)(2,1)S(1)}, u32[]{:S(2)}, u32[]{:S(2)}) %collective-permute-start.1) | collective-permute-done | bytes 55328 | tf_op jit(solution)/shard_map/ppermute | solution.py:516
  11.0 0.0 collective-permute-done
  11.0 4.2 %collective-permute-start.5 = (bf16[4,216,128]{2,1,0:T(8,128)(2,1)S(1)}, bf16[4,216,128]{2,1,0:T(8,128)(2,1)S(1)}, u32[]{:S(2)}, u32[]{:S(2)}) collective-permute-start(bf16[4,216,128]{2,1,0:T(8,128)(2,1)S(1)} %pad_maximum_fusion.refs_0_), channel_id=1, source_target_pairs={{0,3},{1,2},{2,1},{3,0},{4,7},{5,6},{6,5},{7,4},{8,11},{9,10},{10,... | collective-permute-start | bytes 663560 | tf_op jit(solution)/shard_map/ppermute | solution.py:516
  15.2 0.2 collective-permute-start.4
  15.4 0.4 collective-permute-start.3
  15.9 0.0 copy-start
  15.9 1.0 %copy-done = bf16[8,1,4,8,8,128]{5,4,3,2,1,0:T(8,128)(2,1)S(1)} copy-done((bf16[8,1,4,8,8,128]{5,4,3,2,1,0:T(8,128)(2,1)S(1)}, bf16[8,1,4,8,8,128]{5,4,3,2,1,0:T(8,128)(2,1)}, u32[]{:S(2)}) %copy-start) | copy-done | bytes 524312
  16.9 0.0 copy-start.1
  16.9 1.0 %copy-done.1 = bf16[8,1,4,8,8,128]{5,4,3,2,1,0:T(8,128)(2,1)S(1)} copy-done((bf16[8,1,4,8,8,128]{5,4,3,2,1,0:T(8,128)(2,1)S(1)}, bf16[8,1,4,8,8,128]{5,4,3,2,1,0:T(8,128)(2,1)}, u32[]{:S(2)}) %copy-start.1) | copy-done | bytes 524312
  17.9 0.7 %shard_map.50 = (bf16[3,4,10,64,128]{4,3,2,1,0:T(8,128)(2,1)S(1)}, bf16[4,8,64,128]{3,2,1,0:T(8,128)(2,1)S(1)}, bf16[4,8,64,128]{3,2,1,0:T(8,128)(2,1)S(1)}, bf16[384,2048]{1,0:T(8,128)(2,1)S(1)}) custom-call(bf16[8,4,8,8,128]{4,3,2,1,0:T(8,128)(2,1)S(1)} %bitcast.43, bf16[8,4,8,8,128]{4,3,2,1,0:T(8,128)(2,1)S(1)} %bitcast.44), custom_call_target="tpu_custom_call" | custom-call | flops 226492416 | bytes 503316 | tf_op jit(solution)/shard_map/pallas_call | solution.py:161
  18.7 0.5 %collective-permute-done.5.refs_3_ = bf16[4,216,128]{2,1,0:T(8,128)(2,1)S(1)} collective-permute-done((bf16[4,216,128]{2,1,0:T(8,128)(2,1)S(1)}, bf16[4,216,128]{2,1,0:T(8,128)(2,1)S(1)}, u32[]{:S(2)}, u32[]{:S(2)}) %collective-permute-start.5) | collective-permute-done | bytes 221216 | tf_op jit(solution)/shard_map/ppermute | solution.py:516
  19.2 2.3 %collective-permute-done.4.refs_2_ = bf16[4,216,128]{2,1,0:T(8,128)(2,1)S(1)} collective-permute-done((bf16[4,216,128]{2,1,0:T(8,128)(2,1)S(1)}, bf16[4,216,128]{2,1,0:T(8,128)(2,1)S(1)}, u32[]{:S(2)}, u32[]{:S(2)}) %collective-permute-start.4) | collective-permute-done | bytes 221216 | tf_op jit(solution)/shard_map/ppermute | solution.py:516
  21.5 0.0 collective-permute-done.3.refs_1_
  21.5 1.3 %shard_map.52 = (bf16[2,8,64,128]{3,2,1,0:T(8,128)(2,1)S(1)}, f32[3456,128]{1,0:T(8,128)S(1)}, f32[512,128]{1,0:T(8,128)S(1)}) custom-call(bf16[4,216,128]{2,1,0:T(8,128)(2,1)S(1)} %pad_maximum_fusion.refs_0_, bf16[4,216,128]{2,1,0:T(8,128)(2,1)S(1)} %collective-permute-done.3.refs_1_, bf16[4,216,128]{2,1,0:T(8,128)(2,1)S(1)} %collective-permute-done.4.refs_2_, ...), custom_call_target="tpu_custom_call" | custom-call | flops 905969664 | bytes 2013265 | tf_op jit(solution)/shard_map/pallas_call | solution.py:161
  22.8 0.1 collective-permute-start.6
  22.8 1.2 %shard_map.53.mine_high.refs_2_ = bf16[2,8,64,128]{3,2,1,0:T(8,128)(2,1)S(1)} custom-call(f32[3456,128]{1,0:T(8,128)S(1)} %get-tuple-element.32.table.refs_0_, f32[512,128]{1,0:T(8,128)S(1)} %get-tuple-element.33.carried, bf16[3,4,10,64,128]{4,3,2,1,0:T(8,128)(2,1)S(1)} %get-tuple-element.29.refs_4_.shifted, ...), custom_call_target="tpu_custom_call" | custom-call | flops 905969664 | bytes 2013265 | tf_op jit(solution)/shard_map/pallas_call | solution.py:161
  24.0 0.9 %collective-permute-start.7 = (bf16[2,8,64,128]{3,2,1,0:T(8,128)(2,1)S(1)}, bf16[2,8,64,128]{3,2,1,0:T(8,128)(2,1)S(1)}, u32[]{:S(2)}, u32[]{:S(2)}) collective-permute-start(bf16[2,8,64,128]{3,2,1,0:T(8,128)(2,1)S(1)} %shard_map.53.mine_high.refs_2_), channel_id=1, source_target_pairs={{0,16},{16,0},{1,17},{17,1},{2,18},{18,2},{3,19},{19,3},{4,20},{20... | collective-permute-start | bytes 786440 | tf_op jit(solution)/shard_map/ppermute | solution.py:556
  24.9 0.0 collective-permute-done.6.other_first.refs_3_
  24.9 0.4 shard_map.54
  25.3 0.8 %collective-permute-done.7.other_later.refs_4_ = bf16[2,8,64,128]{3,2,1,0:T(8,128)(2,1)S(1)} collective-permute-done((bf16[2,8,64,128]{3,2,1,0:T(8,128)(2,1)S(1)}, bf16[2,8,64,128]{3,2,1,0:T(8,128)(2,1)S(1)}, u32[]{:S(2)}, u32[]{:S(2)}) %collective-permute-start.7) | collective-permute-done | bytes 262176 | tf_op jit(solution)/shard_map/ppermute | solution.py:556
  26.1 2.1 %shard_map.55 = bf16[4,4,216,128]{3,2,1,0:T(8,128)(2,1)S(1)} custom-call(bf16[384,2048]{1,0:T(8,128)(2,1)S(1)} %get-tuple-element.24.ready, f32[4,8,64,128]{3,2,1,0:T(8,128)S(1)} %get-tuple-element.38.slope, bf16[6,10,64,128]{3,2,1,0:T(8,128)(2,1)S(1)} %get-tuple-element.39.moved, bf16[384,1024]{1,0:T(8,128)(2,1)S(1)} %get-tuple-element.40.turned_first, ...), custom_call_target="tpu_custom_call" | custom-call | flops 1811939328 | bytes 4026531 | tf_op jit(solution)/shard_map/pallas_call | solution.py:161
  28.2 2.2 %collective-permute-start.10 = (bf16[4,216,128]{2,1,0:T(8,128)(2,1)S(1)}, bf16[4,216,128]{2,1,0:T(8,128)(2,1)S(1)}, u32[]{:S(2)}, u32[]{:S(2)}) collective-permute-start(bf16[4,216,128]{2,1,0:T(8,128)(2,1)S(1)} %get-tuple-element.48), channel_id=1, source_target_pairs={{0,3},{1,2},{2,1},{3,0},{4,7},{5,6},{6,5},{7,4},{8,11},{9,10},{10,... | collective-permute-start | bytes 663560 | tf_op jit(solution)/shard_map/ppermute | solution.py:516
  30.4 1.4 %collective-permute-start.9 = (bf16[4,216,128]{2,1,0:T(8,128)(2,1)S(1)}, bf16[4,216,128]{2,1,0:T(8,128)(2,1)S(1)}, u32[]{:S(2)}, u32[]{:S(2)}) collective-permute-start(bf16[4,216,128]{2,1,0:T(8,128)(2,1)S(1)} %get-tuple-element.49), channel_id=1, source_target_pairs={{0,2},{1,3},{2,0},{3,1},{4,6},{5,7},{6,4},{7,5},{8,10},{9,11},{10,... | collective-permute-start | bytes 663560 | tf_op jit(solution)/shard_map/ppermute | solution.py:516
  31.8 0.0 collective-permute-start.8
  31.8 0.9 %shard_map.56 = bf16[8,4,8,8,128]{4,3,2,1,0:T(8,128)(2,1)} custom-call(f32[3456,128]{1,0:T(8,128)S(1)} %get-tuple-element.32.table.refs_0_, bf16[2,8,64,128]{3,2,1,0:T(8,128)(2,1)S(1)} %get-tuple-element.31.mine_low.refs_1_, bf16[2,8,64,128]{3,2,1,0:T(8,128)(2,1)S(1)} %shard_map.53.mine_high.refs_2_, ...), custom_call_target="tpu_custom_call" | custom-call | flops 1811939328 | bytes 4026531 | tf_op jit(solution)/shard_map/pallas_call | solution.py:161
  32.7 2.5 %collective-permute-done.10 = bf16[4,216,128]{2,1,0:T(8,128)(2,1)S(1)} collective-permute-done((bf16[4,216,128]{2,1,0:T(8,128)(2,1)S(1)}, bf16[4,216,128]{2,1,0:T(8,128)(2,1)S(1)}, u32[]{:S(2)}, u32[]{:S(2)}) %collective-permute-start.10) | collective-permute-done | bytes 221216 | tf_op jit(solution)/shard_map/ppermute | solution.py:516
  35.3 2.3 %collective-permute-done.9 = bf16[4,216,128]{2,1,0:T(8,128)(2,1)S(1)} collective-permute-done((bf16[4,216,128]{2,1,0:T(8,128)(2,1)S(1)}, bf16[4,216,128]{2,1,0:T(8,128)(2,1)S(1)}, u32[]{:S(2)}, u32[]{:S(2)}) %collective-permute-start.9) | collective-permute-done | bytes 221216 | tf_op jit(solution)/shard_map/ppermute | solution.py:516
  37.5 0.3 collective-permute-done.8
  37.8 0.1 fusion.2
  37.9 0.7 %collective-permute-start.11 = (bf16[216,128]{1,0:T(8,128)(2,1)S(1)}, bf16[216,128]{1,0:T(8,128)(2,1)S(1)}, u32[]{:S(2)}, u32[]{:S(2)}) collective-permute-start(bf16[216,128]{1,0:T(8,128)(2,1)S(1)} %get-tuple-element.51), channel_id=1, source_target_pairs={{0,12},{1,13},{2,14},{3,15},{4,8},{5,9},{6,10},{7,11},{8,4},{9,5},... | collective-permute-start | bytes 165896 | tf_op jit(solution)/shard_map/ppermute | solution.py:516
  38.6 0.8 %collective-permute-start.13 = (bf16[216,128]{1,0:T(8,128)(2,1)S(1)}, bf16[216,128]{1,0:T(8,128)(2,1)S(1)}, u32[]{:S(2)}, u32[]{:S(2)}) collective-permute-start(bf16[216,128]{1,0:T(8,128)(2,1)S(1)} %get-tuple-element.52), channel_id=1, source_target_pairs={{0,4},{1,5},{2,6},{3,7},{4,0},{5,1},{6,2},{7,3},{8,12},{9,13},{10,... | collective-permute-start | bytes 165896 | tf_op jit(solution)/shard_map/ppermute | solution.py:516
  39.4 2.9 %collective-permute-start.12 = (bf16[216,128]{1,0:T(8,128)(2,1)S(1)}, bf16[216,128]{1,0:T(8,128)(2,1)S(1)}, u32[]{:S(2)}, u32[]{:S(2)}) collective-permute-start(bf16[216,128]{1,0:T(8,128)(2,1)S(1)} %get-tuple-element.53), channel_id=1, source_target_pairs={{0,8},{1,9},{2,10},{3,11},{4,12},{5,13},{6,14},{7,15},{8,0},{9,1},... | collective-permute-start | bytes 165896 | tf_op jit(solution)/shard_map/ppermute | solution.py:516
  42.4 1.6 %collective-permute-done.11 = bf16[216,128]{1,0:T(8,128)(2,1)S(1)} collective-permute-done((bf16[216,128]{1,0:T(8,128)(2,1)S(1)}, bf16[216,128]{1,0:T(8,128)(2,1)S(1)}, u32[]{:S(2)}, u32[]{:S(2)}) %collective-permute-start.11) | collective-permute-done | bytes 55328 | tf_op jit(solution)/shard_map/ppermute | solution.py:516
  43.9 0.0 collective-permute-done.13
  43.9 0.6 %collective-permute-done.12 = bf16[216,128]{1,0:T(8,128)(2,1)S(1)} collective-permute-done((bf16[216,128]{1,0:T(8,128)(2,1)S(1)}, bf16[216,128]{1,0:T(8,128)(2,1)S(1)}, u32[]{:S(2)}, u32[]{:S(2)}) %collective-permute-start.12) | collective-permute-done | bytes 55328 | tf_op jit(solution)/shard_map/ppermute | solution.py:516
  44.5 0.7 %fusion.6 = f32[1,216,128]{2,1,0:T(8,128)} fusion(bf16[216,128]{1,0:T(8,128)(2,1)S(1)} %collective-permute-done.13, bf16[216,128]{1,0:T(8,128)(2,1)S(1)} %collective-permute-done.12, bf16[216,128]{1,0:T(8,128)(2,1)S(1)} %collective-permute-done.11, bf16[4,4,216,128]{3,2,1,0:T(8,128)(2,1)S(1)} %shard_map.55, ...), kind=kLoop, calls=%fused_computation.13 | loop fusion | flops 359424 | bytes 497664 | tf_op jit(solution)/shard_map/broadcast_in_dim | solution.py:592
  (4 shorter events, 0.1 us)
Async XLA Ops:
  0.6 7.5 %collective-permute-start.2 = (bf16[216,128]{1,0:T(8,128)(2,1)}, bf16[216,128]{1,0:T(8,128)(2,1)S(1)}, u32[]{:S(2)}, u32[]{:S(2)}) collective-permute-start(bf16[216,128]{1,0:T(8,128)(2,1)} %bitcast.46), channel_id=1, source_target_pairs={{0,12},{1,13},{2,14},{3,15},{4,8},{5,9},{6,10},{7,11},{8,4},{9,5},... | collective-permute-start | bytes 165896 | tf_op jit(solution)/shard_map/ppermute | solution.py:516
  5.7 5.3 %collective-permute-start.1 = (bf16[216,128]{1,0:T(8,128)(2,1)}, bf16[216,128]{1,0:T(8,128)(2,1)S(1)}, u32[]{:S(2)}, u32[]{:S(2)}) collective-permute-start(bf16[216,128]{1,0:T(8,128)(2,1)} %bitcast.47), channel_id=1, source_target_pairs={{0,8},{1,9},{2,10},{3,11},{4,12},{5,13},{6,14},{7,15},{8,0},{9,1},... | collective-permute-start | bytes 165896 | tf_op jit(solution)/shard_map/ppermute | solution.py:516
  5.7 5.3 %collective-permute-start = (bf16[216,128]{1,0:T(8,128)(2,1)}, bf16[216,128]{1,0:T(8,128)(2,1)S(1)}, u32[]{:S(2)}, u32[]{:S(2)}) collective-permute-start(bf16[216,128]{1,0:T(8,128)(2,1)} %bitcast.48), channel_id=1, source_target_pairs={{0,4},{1,5},{2,6},{3,7},{4,0},{5,1},{6,2},{7,3},{8,12},{9,13},{10,... | collective-permute-start | bytes 165896 | tf_op jit(solution)/shard_map/ppermute | solution.py:516
  6.4 0.8 %copy-start.2 = (bf16[1,216,128]{2,1,0:T(8,128)(2,1)S(1)}, bf16[1,216,128]{2,1,0:T(8,128)(2,1)}, u32[]{:S(2)}) copy-start(bf16[1,216,128]{2,1,0:T(8,128)(2,1)} %param.5) | copy-start | bytes 165892
  11.0 8.1 %collective-permute-start.5 = (bf16[4,216,128]{2,1,0:T(8,128)(2,1)S(1)}, bf16[4,216,128]{2,1,0:T(8,128)(2,1)S(1)}, u32[]{:S(2)}, u32[]{:S(2)}) collective-permute-start(bf16[4,216,128]{2,1,0:T(8,128)(2,1)S(1)} %pad_maximum_fusion.refs_0_), channel_id=1, source_target_pairs={{0,3},{1,2},{2,1},{3,0},{4,7},{5,6},{6,5},{7,4},{8,11},{9,10},{10,... | collective-permute-start | bytes 663560 | tf_op jit(solution)/shard_map/ppermute | solution.py:516
  15.2 6.3 %collective-permute-start.4 = (bf16[4,216,128]{2,1,0:T(8,128)(2,1)S(1)}, bf16[4,216,128]{2,1,0:T(8,128)(2,1)S(1)}, u32[]{:S(2)}, u32[]{:S(2)}) collective-permute-start(bf16[4,216,128]{2,1,0:T(8,128)(2,1)S(1)} %pad_maximum_fusion.refs_0_), channel_id=1, source_target_pairs={{0,2},{1,3},{2,0},{3,1},{4,6},{5,7},{6,4},{7,5},{8,10},{9,11},{10,... | collective-permute-start | bytes 663560 | tf_op jit(solution)/shard_map/ppermute | solution.py:516
  15.4 6.1 %collective-permute-start.3 = (bf16[4,216,128]{2,1,0:T(8,128)(2,1)S(1)}, bf16[4,216,128]{2,1,0:T(8,128)(2,1)S(1)}, u32[]{:S(2)}, u32[]{:S(2)}) collective-permute-start(bf16[4,216,128]{2,1,0:T(8,128)(2,1)S(1)} %pad_maximum_fusion.refs_0_), channel_id=1, source_target_pairs={{0,1},{1,0},{2,3},{3,2},{4,5},{5,4},{6,7},{7,6},{8,9},{9,8},{10,11... | collective-permute-start | bytes 663560 | tf_op jit(solution)/shard_map/ppermute | solution.py:516
  15.9 1.0 %copy-start = (bf16[8,1,4,8,8,128]{5,4,3,2,1,0:T(8,128)(2,1)S(1)}, bf16[8,1,4,8,8,128]{5,4,3,2,1,0:T(8,128)(2,1)}, u32[]{:S(2)}) copy-start(bf16[8,1,4,8,8,128]{5,4,3,2,1,0:T(8,128)(2,1)} %param.3) | copy-start | bytes 1572868
  16.9 1.0 %copy-start.1 = (bf16[8,1,4,8,8,128]{5,4,3,2,1,0:T(8,128)(2,1)S(1)}, bf16[8,1,4,8,8,128]{5,4,3,2,1,0:T(8,128)(2,1)}, u32[]{:S(2)}) copy-start(bf16[8,1,4,8,8,128]{5,4,3,2,1,0:T(8,128)(2,1)} %param.4) | copy-start | bytes 1572868
  22.8 2.1 %collective-permute-start.6 = (bf16[2,8,64,128]{3,2,1,0:T(8,128)(2,1)S(1)}, bf16[2,8,64,128]{3,2,1,0:T(8,128)(2,1)S(1)}, u32[]{:S(2)}, u32[]{:S(2)}) collective-permute-start(bf16[2,8,64,128]{3,2,1,0:T(8,128)(2,1)S(1)} %get-tuple-element.31.mine_low.refs_1_), channel_id=1, source_target_pairs={{0,16},{16,0},{1,17},{17,1},{2,18},{18,2},{3,19},{19,3},{4,20},{20... | collective-permute-start | bytes 786440 | tf_op jit(solution)/shard_map/ppermute | solution.py:552
  24.0 2.0 %collective-permute-start.7 = (bf16[2,8,64,128]{3,2,1,0:T(8,128)(2,1)S(1)}, bf16[2,8,64,128]{3,2,1,0:T(8,128)(2,1)S(1)}, u32[]{:S(2)}, u32[]{:S(2)}) collective-permute-start(bf16[2,8,64,128]{3,2,1,0:T(8,128)(2,1)S(1)} %shard_map.53.mine_high.refs_2_), channel_id=1, source_target_pairs={{0,16},{16,0},{1,17},{17,1},{2,18},{18,2},{3,19},{19,3},{4,20},{20... | collective-permute-start | bytes 786440 | tf_op jit(solution)/shard_map/ppermute | solution.py:556
  28.2 7.0 %collective-permute-start.10 = (bf16[4,216,128]{2,1,0:T(8,128)(2,1)S(1)}, bf16[4,216,128]{2,1,0:T(8,128)(2,1)S(1)}, u32[]{:S(2)}, u32[]{:S(2)}) collective-permute-start(bf16[4,216,128]{2,1,0:T(8,128)(2,1)S(1)} %get-tuple-element.48), channel_id=1, source_target_pairs={{0,3},{1,2},{2,1},{3,0},{4,7},{5,6},{6,5},{7,4},{8,11},{9,10},{10,... | collective-permute-start | bytes 663560 | tf_op jit(solution)/shard_map/ppermute | solution.py:516
  30.4 7.1 %collective-permute-start.9 = (bf16[4,216,128]{2,1,0:T(8,128)(2,1)S(1)}, bf16[4,216,128]{2,1,0:T(8,128)(2,1)S(1)}, u32[]{:S(2)}, u32[]{:S(2)}) collective-permute-start(bf16[4,216,128]{2,1,0:T(8,128)(2,1)S(1)} %get-tuple-element.49), channel_id=1, source_target_pairs={{0,2},{1,3},{2,0},{3,1},{4,6},{5,7},{6,4},{7,5},{8,10},{9,11},{10,... | collective-permute-start | bytes 663560 | tf_op jit(solution)/shard_map/ppermute | solution.py:516
  31.8 5.9 %collective-permute-start.8 = (bf16[4,216,128]{2,1,0:T(8,128)(2,1)S(1)}, bf16[4,216,128]{2,1,0:T(8,128)(2,1)S(1)}, u32[]{:S(2)}, u32[]{:S(2)}) collective-permute-start(bf16[4,216,128]{2,1,0:T(8,128)(2,1)S(1)} %get-tuple-element.50), channel_id=1, source_target_pairs={{0,1},{1,0},{2,3},{3,2},{4,5},{5,4},{6,7},{7,6},{8,9},{9,8},{10,11... | collective-permute-start | bytes 663560 | tf_op jit(solution)/shard_map/ppermute | solution.py:516
  37.9 6.0 %collective-permute-start.11 = (bf16[216,128]{1,0:T(8,128)(2,1)S(1)}, bf16[216,128]{1,0:T(8,128)(2,1)S(1)}, u32[]{:S(2)}, u32[]{:S(2)}) collective-permute-start(bf16[216,128]{1,0:T(8,128)(2,1)S(1)} %get-tuple-element.51), channel_id=1, source_target_pairs={{0,12},{1,13},{2,14},{3,15},{4,8},{5,9},{6,10},{7,11},{8,4},{9,5},... | collective-permute-start | bytes 165896 | tf_op jit(solution)/shard_map/ppermute | solution.py:516
  38.6 5.3 %collective-permute-start.13 = (bf16[216,128]{1,0:T(8,128)(2,1)S(1)}, bf16[216,128]{1,0:T(8,128)(2,1)S(1)}, u32[]{:S(2)}, u32[]{:S(2)}) collective-permute-start(bf16[216,128]{1,0:T(8,128)(2,1)S(1)} %get-tuple-element.52), channel_id=1, source_target_pairs={{0,4},{1,5},{2,6},{3,7},{4,0},{5,1},{6,2},{7,3},{8,12},{9,13},{10,... | collective-permute-start | bytes 165896 | tf_op jit(solution)/shard_map/ppermute | solution.py:516
  39.4 5.1 %collective-permute-start.12 = (bf16[216,128]{1,0:T(8,128)(2,1)S(1)}, bf16[216,128]{1,0:T(8,128)(2,1)S(1)}, u32[]{:S(2)}, u32[]{:S(2)}) collective-permute-start(bf16[216,128]{1,0:T(8,128)(2,1)S(1)} %get-tuple-element.53), channel_id=1, source_target_pairs={{0,8},{1,9},{2,10},{3,11},{4,12},{5,13},{6,14},{7,15},{8,0},{9,1},... | collective-permute-start | bytes 165896 | tf_op jit(solution)/shard_map/ppermute | solution.py:516

commit v3 on v2

--- a/solution.py
+++ b/solution.py
@@ -338,8 +338,9 @@
 
     @pl.when(section != 0)
     def _():
-        _, second, third, _, _ = backward_weights(table, channels)
-        part = against(row_patches(shifted, 3, 1, height), [third, second])
+        first, second, third, _, _ = backward_weights(table, channels)
+        part = against(row_patches(shifted, 3, 1, height), [third, second, first])
+        carried[...] = column(part, 2, channels)
         own = against(row_patches(shifted, 2, 1, height), [third])
         for t, branch in enumerate((own + column(part, 1, channels), column(part, 0, channels))):
             result[t] = branch.reshape(height, flat, channels).astype(jnp.bfloat16)
@@ -369,14 +370,13 @@
         parts = [
             against(row_patches(shifted, t, 1, height), weights)
             for t, weights in (
-                (3, [first]),
                 (2, [second, first]),
                 (1, [third, first_two]),
                 (0, [all_three]),
             )
         ]
-        early = column(parts[1], 1, channels) + column(parts[2], 1, channels) + parts[3]
-        later = parts[0] + column(parts[1], 0, channels) + column(parts[2], 0, channels)
+        early = column(parts[0], 1, channels) + column(parts[1], 1, channels) + parts[2]
+        later = carried[...] + column(parts[0], 0, channels) + column(parts[1], 0, channels)
         for t, branch in enumerate((early, later)):
             result[t] = branch.reshape(height, flat, channels).astype(jnp.bfloat16)
 

time: 46 us -> 45.8 us (level)
  no operation moved by 1% of the time
where the time goes in v3:
time: 45.8 us; the launch traced here: 45 us
  starting transfers between devices  19.3 us (42%)
  waiting for transfers between devices  14.7 us (32%)
  Pallas kernels  6.54 us (14%)
  local copies, waits for them, and re-layouts  2.99 us (7%)
  other arithmetic  0.83 us (2%)
  between operations  0.72 us (2%)
    ppermute x12, starting transfers between devices, traded(): return lax.ppermute(block, ('section', 'dp'), route)  18.6 us
    ppermute x12, waiting for transfers between devices, traded(): return lax.ppermute(block, ('section', 'dp'), route)  13.9 us
    pallas_call x7, Pallas kernels, call(): pl.pallas_call(body, out_shape=[jax.ShapeDtypeStruct(shape, dtype) for sh...  6.54 us
    unnamed x6, local copies, waits for them, and re-layouts  2.93 us
  transfers between devices with their start and end apart: 14, of which 10 were waited for; matrix products, arithmetic and copies ran while one was open for 0% of the time, Pallas kernels for 7%

profile of v3, /device:TPU:0, one launch (start us, length us, event | category | flops | bytes accessed | tf_op | source)
XLA Modules:
  0.0 45.0 jit_solution(9435498192410905566)
XLA Ops:
  0.6 5.1 %collective-permute-start.2 = (bf16[216,128]{1,0:T(8,128)(2,1)}, bf16[216,128]{1,0:T(8,128)(2,1)S(1)}, u32[]{:S(2)}, u32[]{:S(2)}) collective-permute-start(bf16[216,128]{1,0:T(8,128)(2,1)} %bitcast.46), channel_id=1, source_target_pairs={{0,12},{1,13},{2,14},{3,15},{4,8},{5,9},{6,10},{7,11},{8,4},{9,5},... | collective-permute-start | bytes 165896 | tf_op jit(solution)/shard_map/ppermute | solution.py:516
  5.7 0.0 collective-permute-start.1
  5.7 0.6 %collective-permute-start = (bf16[216,128]{1,0:T(8,128)(2,1)}, bf16[216,128]{1,0:T(8,128)(2,1)S(1)}, u32[]{:S(2)}, u32[]{:S(2)}) collective-permute-start(bf16[216,128]{1,0:T(8,128)(2,1)} %bitcast.48), channel_id=1, source_target_pairs={{0,4},{1,5},{2,6},{3,7},{4,0},{5,1},{6,2},{7,3},{8,12},{9,13},{10,... | collective-permute-start | bytes 165896 | tf_op jit(solution)/shard_map/ppermute | solution.py:516
  6.4 0.0 copy-start.2
  6.4 0.8 %copy-done.2 = bf16[1,216,128]{2,1,0:T(8,128)(2,1)S(1)} copy-done((bf16[1,216,128]{2,1,0:T(8,128)(2,1)S(1)}, bf16[1,216,128]{2,1,0:T(8,128)(2,1)}, u32[]{:S(2)}) %copy-start.2) | copy-done | bytes 55320
  7.2 0.9 %collective-permute-done.2 = bf16[216,128]{1,0:T(8,128)(2,1)S(1)} collective-permute-done((bf16[216,128]{1,0:T(8,128)(2,1)}, bf16[216,128]{1,0:T(8,128)(2,1)S(1)}, u32[]{:S(2)}, u32[]{:S(2)}) %collective-permute-start.2) | collective-permute-done | bytes 55328 | tf_op jit(solution)/shard_map/ppermute | solution.py:516
  8.1 2.9 %collective-permute-done.1 = bf16[216,128]{1,0:T(8,128)(2,1)S(1)} collective-permute-done((bf16[216,128]{1,0:T(8,128)(2,1)}, bf16[216,128]{1,0:T(8,128)(2,1)S(1)}, u32[]{:S(2)}, u32[]{:S(2)}) %collective-permute-start.1) | collective-permute-done | bytes 55328 | tf_op jit(solution)/shard_map/ppermute | solution.py:516
  11.0 0.0 collective-permute-done
  11.0 4.2 %collective-permute-start.5 = (bf16[4,216,128]{2,1,0:T(8,128)(2,1)S(1)}, bf16[4,216,128]{2,1,0:T(8,128)(2,1)S(1)}, u32[]{:S(2)}, u32[]{:S(2)}) collective-permute-start(bf16[4,216,128]{2,1,0:T(8,128)(2,1)S(1)} %pad_maximum_fusion.refs_0_), channel_id=1, source_target_pairs={{0,3},{1,2},{2,1},{3,0},{4,7},{5,6},{6,5},{7,4},{8,11},{9,10},{10,... | collective-permute-start | bytes 663560 | tf_op jit(solution)/shard_map/ppermute | solution.py:516
  15.2 0.2 collective-permute-start.4
  15.4 0.4 collective-permute-start.3
  15.9 0.0 copy-start
  15.9 1.0 %copy-done = bf16[8,1,4,8,8,128]{5,4,3,2,1,0:T(8,128)(2,1)S(1)} copy-done((bf16[8,1,4,8,8,128]{5,4,3,2,1,0:T(8,128)(2,1)S(1)}, bf16[8,1,4,8,8,128]{5,4,3,2,1,0:T(8,128)(2,1)}, u32[]{:S(2)}) %copy-start) | copy-done | bytes 524312
  16.9 0.0 copy-start.1
  16.9 1.0 %copy-done.1 = bf16[8,1,4,8,8,128]{5,4,3,2,1,0:T(8,128)(2,1)S(1)} copy-done((bf16[8,1,4,8,8,128]{5,4,3,2,1,0:T(8,128)(2,1)S(1)}, bf16[8,1,4,8,8,128]{5,4,3,2,1,0:T(8,128)(2,1)}, u32[]{:S(2)}) %copy-start.1) | copy-done | bytes 524312
  17.9 0.7 %shard_map.50 = (bf16[3,4,10,64,128]{4,3,2,1,0:T(8,128)(2,1)S(1)}, bf16[4,8,64,128]{3,2,1,0:T(8,128)(2,1)S(1)}, bf16[4,8,64,128]{3,2,1,0:T(8,128)(2,1)S(1)}, bf16[384,2048]{1,0:T(8,128)(2,1)S(1)}) custom-call(bf16[8,4,8,8,128]{4,3,2,1,0:T(8,128)(2,1)S(1)} %bitcast.43, bf16[8,4,8,8,128]{4,3,2,1,0:T(8,128)(2,1)S(1)} %bitcast.44), custom_call_target="tpu_custom_call" | custom-call | flops 226492416 | bytes 503316 | tf_op jit(solution)/shard_map/pallas_call | solution.py:161
  18.7 0.5 %collective-permute-done.5.refs_3_ = bf16[4,216,128]{2,1,0:T(8,128)(2,1)S(1)} collective-permute-done((bf16[4,216,128]{2,1,0:T(8,128)(2,1)S(1)}, bf16[4,216,128]{2,1,0:T(8,128)(2,1)S(1)}, u32[]{:S(2)}, u32[]{:S(2)}) %collective-permute-start.5) | collective-permute-done | bytes 221216 | tf_op jit(solution)/shard_map/ppermute | solution.py:516
  19.2 2.3 %collective-permute-done.4.refs_2_ = bf16[4,216,128]{2,1,0:T(8,128)(2,1)S(1)} collective-permute-done((bf16[4,216,128]{2,1,0:T(8,128)(2,1)S(1)}, bf16[4,216,128]{2,1,0:T(8,128)(2,1)S(1)}, u32[]{:S(2)}, u32[]{:S(2)}) %collective-permute-start.4) | collective-permute-done | bytes 221216 | tf_op jit(solution)/shard_map/ppermute | solution.py:516
  21.5 0.0 collective-permute-done.3.refs_1_
  21.5 1.3 %shard_map.52 = (bf16[2,8,64,128]{3,2,1,0:T(8,128)(2,1)S(1)}, f32[3456,128]{1,0:T(8,128)S(1)}, f32[512,128]{1,0:T(8,128)S(1)}) custom-call(bf16[4,216,128]{2,1,0:T(8,128)(2,1)S(1)} %pad_maximum_fusion.refs_0_, bf16[4,216,128]{2,1,0:T(8,128)(2,1)S(1)} %collective-permute-done.3.refs_1_, bf16[4,216,128]{2,1,0:T(8,128)(2,1)S(1)} %collective-permute-done.4.refs_2_, ...), custom_call_target="tpu_custom_call" | custom-call | flops 905969664 | bytes 2013265 | tf_op jit(solution)/shard_map/pallas_call | solution.py:161
  22.8 0.1 collective-permute-start.6
  22.8 1.2 %shard_map.53.mine_high.refs_2_ = bf16[2,8,64,128]{3,2,1,0:T(8,128)(2,1)S(1)} custom-call(f32[3456,128]{1,0:T(8,128)S(1)} %get-tuple-element.32.table.refs_0_, f32[512,128]{1,0:T(8,128)S(1)} %get-tuple-element.33.carried, bf16[3,4,10,64,128]{4,3,2,1,0:T(8,128)(2,1)S(1)} %get-tuple-element.29.refs_4_.shifted, ...), custom_call_target="tpu_custom_call" | custom-call | flops 905969664 | bytes 2013265 | tf_op jit(solution)/shard_map/pallas_call | solution.py:161
  24.0 0.6 %collective-permute-start.7 = (bf16[2,8,64,128]{3,2,1,0:T(8,128)(2,1)S(1)}, bf16[2,8,64,128]{3,2,1,0:T(8,128)(2,1)S(1)}, u32[]{:S(2)}, u32[]{:S(2)}) collective-permute-start(bf16[2,8,64,128]{3,2,1,0:T(8,128)(2,1)S(1)} %shard_map.53.mine_high.refs_2_), channel_id=1, source_target_pairs={{0,16},{16,0},{1,17},{17,1},{2,18},{18,2},{3,19},{19,3},{4,20},{20... | collective-permute-start | bytes 786440 | tf_op jit(solution)/shard_map/ppermute | solution.py:556
  24.6 0.0 collective-permute-done.6.other_first.refs_3_
  24.6 0.4 shard_map.54
  25.0 0.8 %collective-permute-done.7.other_later.refs_4_ = bf16[2,8,64,128]{3,2,1,0:T(8,128)(2,1)S(1)} collective-permute-done((bf16[2,8,64,128]{3,2,1,0:T(8,128)(2,1)S(1)}, bf16[2,8,64,128]{3,2,1,0:T(8,128)(2,1)S(1)}, u32[]{:S(2)}, u32[]{:S(2)}) %collective-permute-start.7) | collective-permute-done | bytes 262176 | tf_op jit(solution)/shard_map/ppermute | solution.py:556
  25.8 2.1 %shard_map.55 = bf16[4,4,216,128]{3,2,1,0:T(8,128)(2,1)S(1)} custom-call(bf16[384,2048]{1,0:T(8,128)(2,1)S(1)} %get-tuple-element.24.ready, f32[4,8,64,128]{3,2,1,0:T(8,128)S(1)} %get-tuple-element.38.slope, bf16[6,10,64,128]{3,2,1,0:T(8,128)(2,1)S(1)} %get-tuple-element.39.moved, bf16[384,1024]{1,0:T(8,128)(2,1)S(1)} %get-tuple-element.40.turned_first, ...), custom_call_target="tpu_custom_call" | custom-call | flops 1811939328 | bytes 4026531 | tf_op jit(solution)/shard_map/pallas_call | solution.py:161
  27.9 2.2 %collective-permute-start.10 = (bf16[4,216,128]{2,1,0:T(8,128)(2,1)S(1)}, bf16[4,216,128]{2,1,0:T(8,128)(2,1)S(1)}, u32[]{:S(2)}, u32[]{:S(2)}) collective-permute-start(bf16[4,216,128]{2,1,0:T(8,128)(2,1)S(1)} %get-tuple-element.48), channel_id=1, source_target_pairs={{0,3},{1,2},{2,1},{3,0},{4,7},{5,6},{6,5},{7,4},{8,11},{9,10},{10,... | collective-permute-start | bytes 663560 | tf_op jit(solution)/shard_map/ppermute | solution.py:516
  30.1 1.4 %collective-permute-start.9 = (bf16[4,216,128]{2,1,0:T(8,128)(2,1)S(1)}, bf16[4,216,128]{2,1,0:T(8,128)(2,1)S(1)}, u32[]{:S(2)}, u32[]{:S(2)}) collective-permute-start(bf16[4,216,128]{2,1,0:T(8,128)(2,1)S(1)} %get-tuple-element.49), channel_id=1, source_target_pairs={{0,2},{1,3},{2,0},{3,1},{4,6},{5,7},{6,4},{7,5},{8,10},{9,11},{10,... | collective-permute-start | bytes 663560 | tf_op jit(solution)/shard_map/ppermute | solution.py:516
  31.5 0.0 collective-permute-start.8
  31.5 0.9 %shard_map.56 = bf16[8,4,8,8,128]{4,3,2,1,0:T(8,128)(2,1)} custom-call(f32[3456,128]{1,0:T(8,128)S(1)} %get-tuple-element.32.table.refs_0_, bf16[2,8,64,128]{3,2,1,0:T(8,128)(2,1)S(1)} %get-tuple-element.31.mine_low.refs_1_, bf16[2,8,64,128]{3,2,1,0:T(8,128)(2,1)S(1)} %shard_map.53.mine_high.refs_2_, ...), custom_call_target="tpu_custom_call" | custom-call | flops 1811939328 | bytes 4026531 | tf_op jit(solution)/shard_map/pallas_call | solution.py:161
  32.4 2.5 %collective-permute-done.10 = bf16[4,216,128]{2,1,0:T(8,128)(2,1)S(1)} collective-permute-done((bf16[4,216,128]{2,1,0:T(8,128)(2,1)S(1)}, bf16[4,216,128]{2,1,0:T(8,128)(2,1)S(1)}, u32[]{:S(2)}, u32[]{:S(2)}) %collective-permute-start.10) | collective-permute-done | bytes 221216 | tf_op jit(solution)/shard_map/ppermute | solution.py:516
  34.9 2.3 %collective-permute-done.9 = bf16[4,216,128]{2,1,0:T(8,128)(2,1)S(1)} collective-permute-done((bf16[4,216,128]{2,1,0:T(8,128)(2,1)S(1)}, bf16[4,216,128]{2,1,0:T(8,128)(2,1)S(1)}, u32[]{:S(2)}, u32[]{:S(2)}) %collective-permute-start.9) | collective-permute-done | bytes 221216 | tf_op jit(solution)/shard_map/ppermute | solution.py:516
  37.2 0.3 collective-permute-done.8
  37.5 0.1 fusion.2
  37.6 1.3 %collective-permute-start.11 = (bf16[216,128]{1,0:T(8,128)(2,1)S(1)}, bf16[216,128]{1,0:T(8,128)(2,1)S(1)}, u32[]{:S(2)}, u32[]{:S(2)}) collective-permute-start(bf16[216,128]{1,0:T(8,128)(2,1)S(1)} %get-tuple-element.51), channel_id=1, source_target_pairs={{0,12},{1,13},{2,14},{3,15},{4,8},{5,9},{6,10},{7,11},{8,4},{9,5},... | collective-permute-start | bytes 165896 | tf_op jit(solution)/shard_map/ppermute | solution.py:516
  38.9 0.2 collective-permute-start.13
  39.1 2.9 %collective-permute-start.12 = (bf16[216,128]{1,0:T(8,128)(2,1)S(1)}, bf16[216,128]{1,0:T(8,128)(2,1)S(1)}, u32[]{:S(2)}, u32[]{:S(2)}) collective-permute-start(bf16[216,128]{1,0:T(8,128)(2,1)S(1)} %get-tuple-element.53), channel_id=1, source_target_pairs={{0,8},{1,9},{2,10},{3,11},{4,12},{5,13},{6,14},{7,15},{8,0},{9,1},... | collective-permute-start | bytes 165896 | tf_op jit(solution)/shard_map/ppermute | solution.py:516
  42.0 1.6 %collective-permute-done.11 = bf16[216,128]{1,0:T(8,128)(2,1)S(1)} collective-permute-done((bf16[216,128]{1,0:T(8,128)(2,1)S(1)}, bf16[216,128]{1,0:T(8,128)(2,1)S(1)}, u32[]{:S(2)}, u32[]{:S(2)}) %collective-permute-start.11) | collective-permute-done | bytes 55328 | tf_op jit(solution)/shard_map/ppermute | solution.py:516
  43.7 0.0 collective-permute-done.13
  43.7 0.6 %collective-permute-done.12 = bf16[216,128]{1,0:T(8,128)(2,1)S(1)} collective-permute-done((bf16[216,128]{1,0:T(8,128)(2,1)S(1)}, bf16[216,128]{1,0:T(8,128)(2,1)S(1)}, u32[]{:S(2)}, u32[]{:S(2)}) %collective-permute-start.12) | collective-permute-done | bytes 55328 | tf_op jit(solution)/shard_map/ppermute | solution.py:516
  44.3 0.7 %fusion.6 = f32[1,216,128]{2,1,0:T(8,128)} fusion(bf16[216,128]{1,0:T(8,128)(2,1)S(1)} %collective-permute-done.13, bf16[216,128]{1,0:T(8,128)(2,1)S(1)} %collective-permute-done.12, bf16[216,128]{1,0:T(8,128)(2,1)S(1)} %collective-permute-done.11, bf16[4,4,216,128]{3,2,1,0:T(8,128)(2,1)S(1)} %shard_map.55, ...), kind=kLoop, calls=%fused_computation.13 | loop fusion | flops 359424 | bytes 497664 | tf_op jit(solution)/shard_map/broadcast_in_dim | solution.py:592
  (4 shorter events, 0.1 us)
Async XLA Ops:
  0.6 7.5 %collective-permute-start.2 = (bf16[216,128]{1,0:T(8,128)(2,1)}, bf16[216,128]{1,0:T(8,128)(2,1)S(1)}, u32[]{:S(2)}, u32[]{:S(2)}) collective-permute-start(bf16[216,128]{1,0:T(8,128)(2,1)} %bitcast.46), channel_id=1, source_target_pairs={{0,12},{1,13},{2,14},{3,15},{4,8},{5,9},{6,10},{7,11},{8,4},{9,5},... | collective-permute-start | bytes 165896 | tf_op jit(solution)/shard_map/ppermute | solution.py:516
  5.7 5.3 %collective-permute-start.1 = (bf16[216,128]{1,0:T(8,128)(2,1)}, bf16[216,128]{1,0:T(8,128)(2,1)S(1)}, u32[]{:S(2)}, u32[]{:S(2)}) collective-permute-start(bf16[216,128]{1,0:T(8,128)(2,1)} %bitcast.47), channel_id=1, source_target_pairs={{0,8},{1,9},{2,10},{3,11},{4,12},{5,13},{6,14},{7,15},{8,0},{9,1},... | collective-permute-start | bytes 165896 | tf_op jit(solution)/shard_map/ppermute | solution.py:516
  5.7 5.3 %collective-permute-start = (bf16[216,128]{1,0:T(8,128)(2,1)}, bf16[216,128]{1,0:T(8,128)(2,1)S(1)}, u32[]{:S(2)}, u32[]{:S(2)}) collective-permute-start(bf16[216,128]{1,0:T(8,128)(2,1)} %bitcast.48), channel_id=1, source_target_pairs={{0,4},{1,5},{2,6},{3,7},{4,0},{5,1},{6,2},{7,3},{8,12},{9,13},{10,... | collective-permute-start | bytes 165896 | tf_op jit(solution)/shard_map/ppermute | solution.py:516
  6.4 0.8 %copy-start.2 = (bf16[1,216,128]{2,1,0:T(8,128)(2,1)S(1)}, bf16[1,216,128]{2,1,0:T(8,128)(2,1)}, u32[]{:S(2)}) copy-start(bf16[1,216,128]{2,1,0:T(8,128)(2,1)} %param.5) | copy-start | bytes 165892
  11.0 8.1 %collective-permute-start.5 = (bf16[4,216,128]{2,1,0:T(8,128)(2,1)S(1)}, bf16[4,216,128]{2,1,0:T(8,128)(2,1)S(1)}, u32[]{:S(2)}, u32[]{:S(2)}) collective-permute-start(bf16[4,216,128]{2,1,0:T(8,128)(2,1)S(1)} %pad_maximum_fusion.refs_0_), channel_id=1, source_target_pairs={{0,3},{1,2},{2,1},{3,0},{4,7},{5,6},{6,5},{7,4},{8,11},{9,10},{10,... | collective-permute-start | bytes 663560 | tf_op jit(solution)/shard_map/ppermute | solution.py:516
  15.2 6.3 %collective-permute-start.4 = (bf16[4,216,128]{2,1,0:T(8,128)(2,1)S(1)}, bf16[4,216,128]{2,1,0:T(8,128)(2,1)S(1)}, u32[]{:S(2)}, u32[]{:S(2)}) collective-permute-start(bf16[4,216,128]{2,1,0:T(8,128)(2,1)S(1)} %pad_maximum_fusion.refs_0_), channel_id=1, source_target_pairs={{0,2},{1,3},{2,0},{3,1},{4,6},{5,7},{6,4},{7,5},{8,10},{9,11},{10,... | collective-permute-start | bytes 663560 | tf_op jit(solution)/shard_map/ppermute | solution.py:516
  15.4 6.1 %collective-permute-start.3 = (bf16[4,216,128]{2,1,0:T(8,128)(2,1)S(1)}, bf16[4,216,128]{2,1,0:T(8,128)(2,1)S(1)}, u32[]{:S(2)}, u32[]{:S(2)}) collective-permute-start(bf16[4,216,128]{2,1,0:T(8,128)(2,1)S(1)} %pad_maximum_fusion.refs_0_), channel_id=1, source_target_pairs={{0,1},{1,0},{2,3},{3,2},{4,5},{5,4},{6,7},{7,6},{8,9},{9,8},{10,11... | collective-permute-start | bytes 663560 | tf_op jit(solution)/shard_map/ppermute | solution.py:516
  15.9 1.0 %copy-start = (bf16[8,1,4,8,8,128]{5,4,3,2,1,0:T(8,128)(2,1)S(1)}, bf16[8,1,4,8,8,128]{5,4,3,2,1,0:T(8,128)(2,1)}, u32[]{:S(2)}) copy-start(bf16[8,1,4,8,8,128]{5,4,3,2,1,0:T(8,128)(2,1)} %param.3) | copy-start | bytes 1572868
  16.9 1.0 %copy-start.1 = (bf16[8,1,4,8,8,128]{5,4,3,2,1,0:T(8,128)(2,1)S(1)}, bf16[8,1,4,8,8,128]{5,4,3,2,1,0:T(8,128)(2,1)}, u32[]{:S(2)}) copy-start(bf16[8,1,4,8,8,128]{5,4,3,2,1,0:T(8,128)(2,1)} %param.4) | copy-start | bytes 1572868
  22.8 1.8 %collective-permute-start.6 = (bf16[2,8,64,128]{3,2,1,0:T(8,128)(2,1)S(1)}, bf16[2,8,64,128]{3,2,1,0:T(8,128)(2,1)S(1)}, u32[]{:S(2)}, u32[]{:S(2)}) collective-permute-start(bf16[2,8,64,128]{3,2,1,0:T(8,128)(2,1)S(1)} %get-tuple-element.31.mine_low.refs_1_), channel_id=1, source_target_pairs={{0,16},{16,0},{1,17},{17,1},{2,18},{18,2},{3,19},{19,3},{4,20},{20... | collective-permute-start | bytes 786440 | tf_op jit(solution)/shard_map/ppermute | solution.py:552
  24.0 1.7 %collective-permute-start.7 = (bf16[2,8,64,128]{3,2,1,0:T(8,128)(2,1)S(1)}, bf16[2,8,64,128]{3,2,1,0:T(8,128)(2,1)S(1)}, u32[]{:S(2)}, u32[]{:S(2)}) collective-permute-start(bf16[2,8,64,128]{3,2,1,0:T(8,128)(2,1)S(1)} %shard_map.53.mine_high.refs_2_), channel_id=1, source_target_pairs={{0,16},{16,0},{1,17},{17,1},{2,18},{18,2},{3,19},{19,3},{4,20},{20... | collective-permute-start | bytes 786440 | tf_op jit(solution)/shard_map/ppermute | solution.py:556
  27.9 7.0 %collective-permute-start.10 = (bf16[4,216,128]{2,1,0:T(8,128)(2,1)S(1)}, bf16[4,216,128]{2,1,0:T(8,128)(2,1)S(1)}, u32[]{:S(2)}, u32[]{:S(2)}) collective-permute-start(bf16[4,216,128]{2,1,0:T(8,128)(2,1)S(1)} %get-tuple-element.48), channel_id=1, source_target_pairs={{0,3},{1,2},{2,1},{3,0},{4,7},{5,6},{6,5},{7,4},{8,11},{9,10},{10,... | collective-permute-start | bytes 663560 | tf_op jit(solution)/shard_map/ppermute | solution.py:516
  30.1 7.1 %collective-permute-start.9 = (bf16[4,216,128]{2,1,0:T(8,128)(2,1)S(1)}, bf16[4,216,128]{2,1,0:T(8,128)(2,1)S(1)}, u32[]{:S(2)}, u32[]{:S(2)}) collective-permute-start(bf16[4,216,128]{2,1,0:T(8,128)(2,1)S(1)} %get-tuple-element.49), channel_id=1, source_target_pairs={{0,2},{1,3},{2,0},{3,1},{4,6},{5,7},{6,4},{7,5},{8,10},{9,11},{10,... | collective-permute-start | bytes 663560 | tf_op jit(solution)/shard_map/ppermute | solution.py:516
  31.5 5.9 %collective-permute-start.8 = (bf16[4,216,128]{2,1,0:T(8,128)(2,1)S(1)}, bf16[4,216,128]{2,1,0:T(8,128)(2,1)S(1)}, u32[]{:S(2)}, u32[]{:S(2)}) collective-permute-start(bf16[4,216,128]{2,1,0:T(8,128)(2,1)S(1)} %get-tuple-element.50), channel_id=1, source_target_pairs={{0,1},{1,0},{2,3},{3,2},{4,5},{5,4},{6,7},{7,6},{8,9},{9,8},{10,11... | collective-permute-start | bytes 663560 | tf_op jit(solution)/shard_map/ppermute | solution.py:516
  37.6 6.1 %collective-permute-start.11 = (bf16[216,128]{1,0:T(8,128)(2,1)S(1)}, bf16[216,128]{1,0:T(8,128)(2,1)S(1)}, u32[]{:S(2)}, u32[]{:S(2)}) collective-permute-start(bf16[216,128]{1,0:T(8,128)(2,1)S(1)} %get-tuple-element.51), channel_id=1, source_target_pairs={{0,12},{1,13},{2,14},{3,15},{4,8},{5,9},{6,10},{7,11},{8,4},{9,5},... | collective-permute-start | bytes 165896 | tf_op jit(solution)/shard_map/ppermute | solution.py:516
  38.9 4.8 %collective-permute-start.13 = (bf16[216,128]{1,0:T(8,128)(2,1)S(1)}, bf16[216,128]{1,0:T(8,128)(2,1)S(1)}, u32[]{:S(2)}, u32[]{:S(2)}) collective-permute-start(bf16[216,128]{1,0:T(8,128)(2,1)S(1)} %get-tuple-element.52), channel_id=1, source_target_pairs={{0,4},{1,5},{2,6},{3,7},{4,0},{5,1},{6,2},{7,3},{8,12},{9,13},{10,... | collective-permute-start | bytes 165896 | tf_op jit(solution)/shard_map/ppermute | solution.py:516
  39.1 5.1 %collective-permute-start.12 = (bf16[216,128]{1,0:T(8,128)(2,1)S(1)}, bf16[216,128]{1,0:T(8,128)(2,1)S(1)}, u32[]{:S(2)}, u32[]{:S(2)}) collective-permute-start(bf16[216,128]{1,0:T(8,128)(2,1)S(1)} %get-tuple-element.53), channel_id=1, source_target_pairs={{0,8},{1,9},{2,10},{3,11},{4,12},{5,13},{6,14},{7,15},{8,0},{9,1},... | collective-permute-start | bytes 165896 | tf_op jit(solution)/shard_map/ppermute | solution.py:516
